TPU v7x, 512 devices: a whole 4x4x16 slice. The times are simulated.
512 devices in a mesh: grid: 64 (over x_lo, z, core), dp: 8 (over y, x_hi).
Axes of the slice: x: 4 (x_hi: 2, x_lo: 2; x = x_hi * 2 + x_lo), y: 4, z: 16, core: 2. Of those that a mesh axis runs over, the one named last changes fastest.
Arguments:
- in_field: bfloat16 [8, 512, 64, 512], P('dp', 'grid'), may hold values from -6 to 6
- out_grad: bfloat16 [8, 512, 64, 512], P('dp', 'grid'), may hold values from -6 to 6
- point_weight: bfloat16 [64, 64], replicated, may hold values from -0.75 to 0.75
- point_bias: float32 [64], replicated, may hold values from -3 to 3
- spectral_weight: float32 [64, 64, 2, 4096], P('dp', 'grid'), may hold values from -3 to 3
- first_moment: float32 [64, 64, 2, 4096], P('dp', 'grid'), may hold values from -8 to 8
- second_moment: float32 [64, 64, 2, 4096], P('dp', 'grid'), may hold values from 1 to 40
Outputs:
- grad_field: bfloat16 [8, 512, 64, 512], P('dp', 'grid')
- new_weight: float32 [64, 64, 2, 4096], P('dp', 'grid')
- new_first: float32 [64, 64, 2, 4096], P('dp', 'grid')
- new_second: float32 [64, 64, 2, 4096], P('dp', 'grid')
All inputs are finite; a program needn't handle non-finite values.
Results may differ from a plain program's by a relative error of at most 0.019.
Values may be sent and summed in bfloat16 or wider, within the bound.
No kernel may reach another device: no remote copies, remote signals or barrier semaphores. Data moves between devices by JAX's collectives and lax.ppermute only.
A program may use at most 128 MiB of HBM per device.

v0:
```python
import math

import jax
import jax.numpy as jnp
from jax import lax
from jax.sharding import PartitionSpec as P

C = 64
NX = 512
NY = 512
MX = 64
MY = 64


beta_one = 0.9
beta_two = 0.999
learn_rate = 0.01
adam_step = 100
epsilon_adam = 1e-08


def row_tables():
    frequency = jnp.arange(MY, dtype=jnp.int32)
    position = jnp.arange(NY, dtype=jnp.int32)
    angles = (position[:, None] * frequency[None, :] % NY).astype(jnp.float32) * (
        2.0 * math.pi / NY
    )
    forward = (
        jnp.stack([jnp.cos(angles), -jnp.sin(angles)], axis=-1)
        .reshape(NY, 2 * MY)
        .astype(jnp.bfloat16)
    )
    factor = jnp.where(frequency == 0, 1.0, 2.0).astype(jnp.float32) / (NX * NY)
    inverse = jnp.stack([factor * jnp.cos(angles), -factor * jnp.sin(angles)], axis=-1)
    inverse = inverse.reshape(NY, 2 * MY).T.astype(jnp.bfloat16)
    return (forward, inverse)


def column_tables():
    column = jnp.arange(MX, dtype=jnp.int32)
    wavenumber = jnp.where(column < MX // 2, column, NX - MX + column)
    position = jnp.arange(NX, dtype=jnp.int32)
    angles = (wavenumber[:, None] * position[None, :] % NX).astype(jnp.float32) * (
        2.0 * math.pi / NX
    )
    return (jnp.cos(angles).astype(jnp.bfloat16), jnp.sin(angles).astype(jnp.bfloat16))


def gelu_slope(value):
    return 0.5 * (1.0 + lax.erf(value / math.sqrt(2.0))) + value * jnp.exp(
        -0.5 * value * value
    ) / math.sqrt(2.0 * math.pi)


def mix_forward(coefficients, weight):
    real_out = jnp.einsum(
        "bqkc,kqco->bqko",
        coefficients[:, :, 0],
        weight[:, :, 0],
        preferred_element_type=jnp.float32,
    )
    real_out = real_out - jnp.einsum(
        "bqkc,kqco->bqko",
        coefficients[:, :, 1],
        weight[:, :, 1],
        preferred_element_type=jnp.float32,
    )
    imaginary_out = jnp.einsum(
        "bqkc,kqco->bqko",
        coefficients[:, :, 0],
        weight[:, :, 1],
        preferred_element_type=jnp.float32,
    )
    imaginary_out = imaginary_out + jnp.einsum(
        "bqkc,kqco->bqko",
        coefficients[:, :, 1],
        weight[:, :, 0],
        preferred_element_type=jnp.float32,
    )
    return jnp.stack([real_out, imaginary_out], axis=2).astype(jnp.bfloat16)


def mix_backward(cotangent, weight):
    real_out = jnp.einsum(
        "bqko,kqco->bqkc", cotangent[:, :, 0], weight[:, :, 0], preferred_element_type=jnp.float32
    )
    real_out = real_out + jnp.einsum(
        "bqko,kqco->bqkc", cotangent[:, :, 1], weight[:, :, 1], preferred_element_type=jnp.float32
    )
    imaginary_out = jnp.einsum(
        "bqko,kqco->bqkc", cotangent[:, :, 1], weight[:, :, 0], preferred_element_type=jnp.float32
    )
    imaginary_out = imaginary_out - jnp.einsum(
        "bqko,kqco->bqkc", cotangent[:, :, 0], weight[:, :, 1], preferred_element_type=jnp.float32
    )
    return jnp.stack([real_out, imaginary_out], axis=2).astype(jnp.bfloat16)


def weight_grad(coefficients, cotangent):
    real_out = jnp.einsum(
        "bqkc,bqko->kqco",
        coefficients[:, :, 0],
        cotangent[:, :, 0],
        preferred_element_type=jnp.float32,
    )
    real_out = real_out + jnp.einsum(
        "bqkc,bqko->kqco",
        coefficients[:, :, 1],
        cotangent[:, :, 1],
        preferred_element_type=jnp.float32,
    )
    imaginary_out = jnp.einsum(
        "bqkc,bqko->kqco",
        coefficients[:, :, 0],
        cotangent[:, :, 1],
        preferred_element_type=jnp.float32,
    )
    imaginary_out = imaginary_out - jnp.einsum(
        "bqkc,bqko->kqco",
        coefficients[:, :, 1],
        cotangent[:, :, 0],
        preferred_element_type=jnp.float32,
    )
    stacked = jnp.stack([real_out, imaginary_out], axis=2)
    return stacked.reshape(stacked.shape[0], stacked.shape[1], 2, C * C)


def shards(
    in_field, out_grad, point_weight, point_bias, spectral_weight, first_moment, second_moment
):
    groups = lax.axis_size("grid")
    batch_size = in_field.shape[0]
    slab_rows = in_field.shape[1]
    mode_cols = spectral_weight.shape[1]
    row_forward, row_inverse = row_tables()
    col_cos, col_sin = column_tables()
    cos_turned = jnp.transpose(col_cos.reshape(MX, groups, slab_rows), (1, 2, 0))
    sin_turned = jnp.transpose(col_sin.reshape(MX, groups, slab_rows), (1, 2, 0))
    forward_block = jnp.stack(
        [jnp.stack([cos_turned, sin_turned], axis=0), jnp.stack([-sin_turned, cos_turned], axis=0)],
        axis=0,
    )
    inverse_block = jnp.stack(
        [jnp.stack([cos_turned, -sin_turned], axis=2), jnp.stack([sin_turned, cos_turned], axis=2)],
        axis=0,
    )

    def to_modes(columns):
        split_parts = columns.reshape(batch_size, mode_cols, 2, groups, slab_rows, C)
        return jnp.einsum(
            "bqpgrc,opgrk->bqokc", split_parts, forward_block, preferred_element_type=jnp.float32
        ).astype(jnp.bfloat16)

    def to_rows(coefficients):
        rows_out = jnp.einsum(
            "bqpkc,ogrpk->bqogrc", coefficients, inverse_block, preferred_element_type=jnp.float32
        ).astype(jnp.bfloat16)
        return rows_out.reshape(batch_size, 2 * mode_cols, groups * slab_rows * C)

    spectra = jnp.einsum(
        "brcy,yj->bjrc", in_field, row_forward, preferred_element_type=jnp.float32
    ).astype(jnp.bfloat16)
    spectra = spectra.reshape(batch_size, 2 * MY, slab_rows * C)
    columns = lax.all_to_all(spectra, "grid", split_axis=1, concat_axis=2, tiled=True)
    field_modes = to_modes(columns)
    local_weight = spectral_weight.astype(jnp.bfloat16)
    full_weight = lax.all_gather(local_weight, "dp", axis=0, tiled=True).reshape(
        MX, mode_cols, 2, C, C
    )
    mixed_modes = mix_forward(field_modes, full_weight)
    returned = lax.all_to_all(to_rows(mixed_modes), "grid", split_axis=2, concat_axis=1, tiled=True)
    returned = returned.reshape(batch_size, 2 * MY, slab_rows, C)
    spectral_out = jnp.einsum(
        "bjrc,jy->brcy", returned, row_inverse, preferred_element_type=jnp.float32
    )
    linear = jnp.einsum("brcy,co->broy", in_field, point_weight, preferred_element_type=jnp.float32)
    pre_activation = spectral_out + linear + point_bias[None, None, :, None]
    pre_grad = (out_grad.astype(jnp.float32) * gelu_slope(pre_activation)).astype(jnp.bfloat16)
    back_spectra = jnp.einsum(
        "broy,jy->bjro", pre_grad, row_inverse, preferred_element_type=jnp.float32
    ).astype(jnp.bfloat16)
    back_spectra = back_spectra.reshape(batch_size, 2 * MY, slab_rows * C)
    back_columns = lax.all_to_all(back_spectra, "grid", split_axis=1, concat_axis=2, tiled=True)
    back_modes = to_modes(back_columns)
    input_modes = mix_backward(back_modes, full_weight)
    gradient = lax.psum_scatter(
        weight_grad(field_modes, back_modes).astype(jnp.bfloat16),
        "dp",
        scatter_dimension=0,
        tiled=True,
    ).astype(jnp.float32)
    input_rows = lax.all_to_all(
        to_rows(input_modes), "grid", split_axis=2, concat_axis=1, tiled=True
    )
    input_rows = input_rows.reshape(batch_size, 2 * MY, slab_rows, C)
    grad_field = jnp.einsum(
        "broy,co->brcy", pre_grad, point_weight, preferred_element_type=jnp.float32
    )
    grad_field = grad_field + jnp.einsum(
        "bjrc,yj->brcy", input_rows, row_forward, preferred_element_type=jnp.float32
    )
    grad_field = grad_field.astype(jnp.bfloat16)
    new_first = beta_one * first_moment + (1.0 - beta_one) * gradient
    new_second = beta_two * second_moment + (1.0 - beta_two) * gradient * gradient
    bias_one = 1.0 - beta_one**adam_step
    bias_two = 1.0 - beta_two**adam_step
    update = learn_rate * (new_first / bias_one) / (jnp.sqrt(new_second / bias_two) + epsilon_adam)
    new_weight = spectral_weight - update
    return (grad_field, new_weight, new_first, new_second)


def solution(mesh):
    return jax.shard_map(
        shards,
        mesh=mesh,
        in_specs=(
            P("dp", "grid", None, None),
            P("dp", "grid", None, None),
            P(),
            P(),
            P("dp", "grid", None, None),
            P("dp", "grid", None, None),
            P("dp", "grid", None, None),
        ),
        out_specs=(
            P("dp", "grid", None, None),
            P("dp", "grid", None, None),
            P("dp", "grid", None, None),
            P("dp", "grid", None, None),
        ),
        check_vma=False,
    )
```

profile of v0, /device:TPU:1, one launch (start us, length us, event | category | flops | bytes accessed | tf_op | source)
XLA Modules:
  0.0 768.9 jit_solution(6188690637746361417)
XLA Ops:
  7.2 0.5 negate_convert_fusion
  8.0 0.3 copy-done
  8.2 0.3 convolution_convert_fusion.1
  8.7 0.5 broadcast.475
  9.2 1.4 reduce.4
  10.6 0.7 reshape.557
  11.3 18.1 %all-to-all-start = ((bf16[64,2,512]{2,1,0:T(2,128)(2,1)}), bf16[64,2,512]{2,1,0:T(2,128)(2,1)S(1)}, u32[]{:S(2)}, u32[]{:S(2)}) async-start(bf16[64,2,512]{2,1,0:T(2,128)(2,1)} %reshape.557), calls=%async_computation | async-start | bytes 262144 | tf_op jit(solution)/shard_map/all_to_all | solution.py:164
  29.4 0.3 all-gather.2.cloned.1.call-start
  29.8 0.7 convert_element_type.210
  30.6 1.0 fusion.65
  31.6 1.2 sine_convert_fusion
  32.9 1.0 fusion.64
  34.1 1.2 sine_convert_fusion.1
  35.5 11.1 %all-to-all-done = bf16[64,2,512]{2,1,0:T(2,128)(2,1)S(1)} async-done(((bf16[64,2,512]{2,1,0:T(2,128)(2,1)}), bf16[64,2,512]{2,1,0:T(2,128)(2,1)S(1)}, u32[]{:S(2)}, u32[]{:S(2)}) %all-to-all-start) | async-done | bytes 131104 | tf_op jit(solution)/shard_map/all_to_all | solution.py:164
  46.7 0.7 bitcast_reduce_fusion.1
  47.7 0.4 fusion.9
  48.1 0.6 bitcast_convert_fusion.3
  48.7 45.7 %all-gather.2.cloned.1.call-done = bf16[64,1,2,4096]{3,2,1,0:T(2,128)(2,1)} async-done(((bf16[8,1,2,4096]{3,2,1,0:T(2,128)(2,1)}), bf16[64,1,2,4096]{3,2,1,0:T(2,128)(2,1)}) %all-gather.2.cloned.1.call-update) | async-done | bytes 1048592 | tf_op jit(solution)/shard_map/all_gather | solution.py:167
  94.4 3.8 reshape.512
  98.2 1.1 fusion.24
  99.3 1.1 fusion.19
  100.4 0.4 fusion.20
  100.8 0.4 fusion.23
  101.3 0.3 fusion.4
  101.8 0.2 reshape.516
  102.0 25.4 %copy.70 = bf16[1,2,32768]{1,0,2:T(2,128)(2,1)} copy(bf16[1,2,32768]{2,1,0:T(2,128)(2,1)S(1)} %reshape.516) | data formatting | bytes 262144 | tf_op jit(solution)/shard_map/reshape | solution.py:158
  127.4 179.7 %reduce.5 = bf16[32768,2]{1,0:T(8,128)(2,1)} reduce(bf16[32768,1,2]{2,1,0:T(2,128)(2,1)} %bitcast.211, bf16[]{:T(256)} %broadcast.475), dimensions={1}, to_apply=%bitcast.196.reduce_sub_computation | reduce | bytes 262146
  307.1 13.7 %reshape.559 = bf16[64,2,512]{2,1,0:T(2,128)(2,1)} reshape(bf16[32768,2]{1,0:T(8,128)(2,1)} %reduce.5) | data formatting | bytes 262144
  320.7 14.8 %all-to-all-start.1 = ((bf16[64,2,512]{2,1,0:T(2,128)(2,1)}), bf16[64,2,512]{2,1,0:T(2,128)(2,1)S(1)}, u32[]{:S(2)}, u32[]{:S(2)}) async-start(bf16[64,2,512]{2,1,0:T(2,128)(2,1)} %reshape.559), calls=%async_computation.1 | async-start | bytes 262144 | tf_op jit(solution)/shard_map/all_to_all | solution.py:171
  335.7 0.6 multiply_convert_fusion
  336.4 16.3 %all-to-all-done.1 = bf16[64,2,512]{2,1,0:T(2,128)(2,1)S(1)} async-done(((bf16[64,2,512]{2,1,0:T(2,128)(2,1)}), bf16[64,2,512]{2,1,0:T(2,128)(2,1)S(1)}, u32[]{:S(2)}, u32[]{:S(2)}) %all-to-all-start.1) | async-done | bytes 131104 | tf_op jit(solution)/shard_map/all_to_all | solution.py:171
  352.7 32.5 %reshape.560 = bf16[32768,1,2]{2,1,0:T(2,128)(2,1)} reshape(bf16[64,2,512]{2,1,0:T(2,128)(2,1)S(1)} %all-to-all-done.1) | data formatting | bytes 262144
  385.2 30.6 %copy.71 = bf16[1,2,32768]{2,1,0:T(2,128)(2,1)S(1)} copy(bf16[1,2,32768]{1,0,2:T(2,128)(2,1)} %bitcast.212) | data formatting | bytes 262144 | tf_op jit(solution)/shard_map/all_to_all | solution.py:171
  416.2 0.3 convolution_bitcast_fusion.3
  416.5 0.3 copy-done.18
  416.9 0.7 fusion.16
  417.6 0.3 convolution_convert_fusion
  418.1 1.4 reduce.6
  419.6 21.0 %all_to_all.60 = bf16[64,2,512]{2,1,0:T(2,128)(2,1)S(1)} all-to-all(bf16[64,2,512]{2,1,0:T(2,128)(2,1)S(1)} %reshape.561), channel_id=1, replica_groups=mesh['grid'=64,'dp'=8] {'grid'}, dimensions={0} | all-to-all | bytes 262144 | tf_op jit(solution)/shard_map/all_to_all | solution.py:183
  440.7 0.7 bitcast_reduce_fusion
  441.7 0.4 fusion.8
  442.1 0.6 bitcast_convert_fusion.1
  442.7 2.0 add_convert_fusion
  444.7 0.8 stack.95
  445.5 0.8 stack.96
  446.5 1.1 copy.131
  447.6 1.6 copy.137
  449.2 0.6 fusion.22
  449.8 1.4 fusion.18
  451.3 1.4 fusion.21
  452.6 0.7 fusion.17
  453.3 0.3 fusion.5
  454.1 25.4 %copy.82 = bf16[1,2,32768]{1,0,2:T(2,128)(2,1)} copy(bf16[1,2,32768]{2,1,0:T(2,128)(2,1)S(1)} %reshape.523) | data formatting | bytes 262144 | tf_op jit(solution)/shard_map/reshape | solution.py:158
  479.5 179.3 %reduce.7 = bf16[32768,2]{1,0:T(8,128)(2,1)} reduce(bf16[32768,1,2]{2,1,0:T(2,128)(2,1)} %bitcast.210, bf16[]{:T(256)} %broadcast.475), dimensions={1}, to_apply=%bitcast.200.reduce_sub_computation | reduce | bytes 262146
  658.8 13.1 %reshape.563 = bf16[64,2,512]{2,1,0:T(2,128)(2,1)S(1)} reshape(bf16[32768,2]{1,0:T(8,128)(2,1)} %reduce.7) | data formatting | bytes 262144
  671.9 20.9 %all_to_all.61 = bf16[64,2,512]{2,1,0:T(2,128)(2,1)S(1)} all-to-all(bf16[64,2,512]{2,1,0:T(2,128)(2,1)S(1)} %reshape.563), channel_id=1, replica_groups=mesh['grid'=64,'dp'=8] {'grid'}, dimensions={0} | all-to-all | bytes 262144 | tf_op jit(solution)/shard_map/all_to_all | solution.py:192
  692.8 32.5 %reshape.564 = bf16[32768,1,2]{2,1,0:T(2,128)(2,1)} reshape(bf16[64,2,512]{2,1,0:T(2,128)(2,1)S(1)} %all_to_all.61) | data formatting | bytes 262144
  725.3 30.6 %copy.83 = bf16[1,2,32768]{2,1,0:T(2,128)(2,1)S(1)} copy(bf16[1,2,32768]{1,0,2:T(2,128)(2,1)} %bitcast.213) | data formatting | bytes 262144 | tf_op jit(solution)/shard_map/all_to_all | solution.py:192
  756.2 0.3 convolution_bitcast_fusion.1
  756.6 1.1 fusion.3
  757.7 1.5 copy_subtract_fusion
  759.1 0.9 copy.90
  760.0 0.9 copy.91
  760.9 0.9 copy.92
  (77 shorter events, 3.5 us)
Async XLA Ops:
  7.2 1.1 copy-start
  7.2 22.6 %copy-start.4 = (f32[8,1,2,4096]{3,2,1,0:T(2,128)S(1)}, f32[8,1,2,4096]{3,2,1,0:T(2,128)}, u32[]{:S(2)}) copy-start(f32[8,1,2,4096]{3,2,1,0:T(2,128)} %param.11) | copy-start | bytes 786436
  11.3 35.2 %all-to-all-start = ((bf16[64,2,512]{2,1,0:T(2,128)(2,1)}), bf16[64,2,512]{2,1,0:T(2,128)(2,1)S(1)}, u32[]{:S(2)}, u32[]{:S(2)}) async-start(bf16[64,2,512]{2,1,0:T(2,128)(2,1)} %reshape.557), calls=%async_computation | async-start | bytes 262144 | tf_op jit(solution)/shard_map/all_to_all | solution.py:164
  29.4 65.0 %all-gather.2.cloned.1.call-start = ((), (), s32[]{:S(2)}) async-start(), calls=%async_computation.5 | async-start | bytes 1179648 | tf_op jit(solution)/shard_map/all_gather | solution.py:167
  34.1 14.6 %copy-start.9 = (bf16[1,2,64,8,64]{2,4,3,0,1:T(8,128)(2,1)}, bf16[1,2,64,8,64]{2,4,3,0,1:T(8,128)(2,1)S(1)}, u32[]{:S(2)}) copy-start(bf16[1,2,64,8,64]{2,4,3,0,1:T(8,128)(2,1)S(1)} %get-tuple-element.21) | copy-start | bytes 393220
  34.1 14.6 %copy-start.11 = (bf16[1,2,64,8,64]{2,4,3,0,1:T(8,128)(2,1)}, bf16[1,2,64,8,64]{2,4,3,0,1:T(8,128)(2,1)S(1)}, u32[]{:S(2)}) copy-start(bf16[1,2,64,8,64]{2,4,3,0,1:T(8,128)(2,1)S(1)} %get-tuple-element.22) | copy-start | bytes 393220
  35.5 65.8 %copy-start.5 = (bf16[1,64,8,2,64]{4,1,3,2,0:T(8,128)(2,1)}, bf16[1,64,8,2,64]{4,1,3,2,0:T(8,128)(2,1)S(1)}, u32[]{:S(2)}) copy-start(bf16[1,64,8,2,64]{4,1,3,2,0:T(8,128)(2,1)S(1)} %get-tuple-element.23) | copy-start | bytes 393220
  35.5 65.8 %copy-start.7 = (bf16[1,64,8,2,64]{4,1,3,2,0:T(8,128)(2,1)}, bf16[1,64,8,2,64]{4,1,3,2,0:T(8,128)(2,1)S(1)}, u32[]{:S(2)}) copy-start(bf16[1,64,8,2,64]{4,1,3,2,0:T(8,128)(2,1)S(1)} %get-tuple-element.24) | copy-start | bytes 393220
  98.2 3.0 copy-start.2
  320.7 32.0 %all-to-all-start.1 = ((bf16[64,2,512]{2,1,0:T(2,128)(2,1)}), bf16[64,2,512]{2,1,0:T(2,128)(2,1)S(1)}, u32[]{:S(2)}, u32[]{:S(2)}) async-start(bf16[64,2,512]{2,1,0:T(2,128)(2,1)} %reshape.559), calls=%async_computation.1 | async-start | bytes 262144 | tf_op jit(solution)/shard_map/all_to_all | solution.py:171
  335.6 422.1 %reduce-scatter.4.cloned.1.call-start = ((), (), s32[]{:S(2)}) async-start(), calls=%async_computation.6 | async-start | bytes 1179648
  415.8 0.8 copy-start.15
  415.8 1.1 copy-start.18
  415.8 1.0 copy-start.19
  417.6 24.1 %copy-start.10 = (bf16[1,2,64,8,64]{2,4,3,0,1:T(8,128)(2,1)S(1)}, bf16[1,2,64,8,64]{2,4,3,0,1:T(8,128)(2,1)}, u32[]{:S(2)}) copy-start(bf16[1,2,64,8,64]{2,4,3,0,1:T(8,128)(2,1)} %copy-done.9) | copy-start | bytes 393220
  417.6 24.1 %copy-start.12 = (bf16[1,2,64,8,64]{2,4,3,0,1:T(8,128)(2,1)S(1)}, bf16[1,2,64,8,64]{2,4,3,0,1:T(8,128)(2,1)}, u32[]{:S(2)}) copy-start(bf16[1,2,64,8,64]{2,4,3,0,1:T(8,128)(2,1)} %copy-done.11) | copy-start | bytes 393220
  447.6 1.6 copy-start.3
  447.6 1.6 copy-start.16
  449.2 3.5 copy-start.17
  449.8 3.5 copy-start.6
  449.8 3.5 copy-start.8
  755.9 1.8 copy-start.13
  755.9 1.8 copy-start.14
  756.6 5.3 copy-start.1
Sparse Core Ops, SparseCore 0:
  33.5 60.8 all-gather.1
  449.3 75.0 reduce-scatter.3
where the time goes:
time: 774 us; the launch traced here: 769 us
  other arithmetic  373 us (48%)
  local copies, waits for them, and re-layouts  221 us (29%)
  waiting for transfers between devices  73.1 us (9%)
  blocking collectives  41.9 us (5%)
  starting transfers between devices  33.3 us (4%)
  between operations  14.9 us (2%)
  matrix products  11.4 us (1%)
    unnamed x4, other arithmetic  362 us
    unnamed x56, local copies, waits for them, and re-layouts  99.3 us
    reshape x4, local copies, waits for them, and re-layouts, to_rows(): return rows_out.reshape(batch_size, 2 * mode_cols, groups * slab_rows * C)  51.2 us
    all_gather x1, waiting for transfers between devices, shards(): lax.all_gather(local_weight, 'dp', axis=0, tiled=True)  45.7 us
    all_to_all x2, local copies, waits for them, and re-layouts, shards(): lax.all_to_all(to_rows(input_modes), 'grid', split_axis=2, concat_axis=1,...  30.7 us
    all_to_all x2, local copies, waits for them, and re-layouts, shards(): lax.all_to_all(to_rows(mixed_modes), 'grid', split_axis=2, concat_axis=1,...  30.7 us
    all_to_all x1, blocking collectives, shards(): lax.all_to_all(back_spectra, 'grid', split_axis=1, concat_axis=2, tiled=T...  21 us
    all_to_all x1, blocking collectives, shards(): lax.all_to_all(to_rows(input_modes), 'grid', split_axis=2, concat_axis=1,...  20.9 us
  transfers between devices with their start and end apart: 4, of which 3 were waited for; matrix products, arithmetic and copies ran while one was open for 38% of the time, Pallas kernels for 0%

commit v1 on v0

v1 whole, which is shorter than its diff:
```python
import math

import jax
import jax.numpy as jnp
import numpy as np
from jax import lax
from jax.experimental import pallas as pl
from jax.experimental.pallas import tpu as pltpu
from jax.sharding import PartitionSpec as P

C = 64
NX = 512
NY = 512
MX = 64
MY = 64
SLAB = 8
QUAD = 4
HALF = 64
BLOCKS = 8

beta_one = 0.9
beta_two = 0.999
learn_rate = 0.01
adam_step = 100
epsilon_adam = 1e-08

f32 = jnp.float32
bf16 = jnp.bfloat16


def tables():
    frequency = np.arange(MY)
    position = np.arange(NY)
    angles = ((position[:, None] * frequency[None, :]) % NY).astype(np.float32) * np.float32(
        2.0 * math.pi / NY
    )
    cos, sin = np.cos(angles), np.sin(angles)
    forward = np.stack([cos, -sin], axis=-1).reshape(NY, 2 * MY).T
    factor = np.where(frequency == 0, 1.0, 2.0).astype(np.float32) / np.float32(NX * NY)
    inverse = np.stack([factor * cos, -factor * sin], axis=-1).reshape(NY, 2 * MY).T

    column = np.arange(MX)
    wavenumber = np.where(column < MX // 2, column, NX - MX + column)
    rows = np.arange(NX)
    turn = ((wavenumber[:, None] * rows[None, :]) % NX).astype(np.float32) * np.float32(
        2.0 * math.pi / NX
    )
    col_cos, col_sin = np.cos(turn), np.sin(turn)

    by_slab = lambda t: t.reshape(BLOCKS, 8, NX // SLAB, QUAD, 2)
    c, s = by_slab(col_cos), by_slab(col_sin)
    to_modes = np.stack([np.stack([c, s], 0), np.stack([-s, c], 0)], 0)
    to_modes = to_modes.transpose(6, 2, 0, 3, 4, 1, 5).reshape(256, 512)

    by_slab = lambda t: t.reshape(MX, NX // SLAB, QUAD, 2)
    c, s = by_slab(col_cos), by_slab(col_sin)
    to_rows = np.stack([np.stack([c, -s], 0), np.stack([s, c], 0)], 0)
    to_rows = to_rows.transpose(3, 0, 4, 1, 5, 2).reshape(512, 256)

    weave = np.eye(512, dtype=np.float32).reshape(QUAD, 128, 512).transpose(1, 0, 2).reshape(512, 512)

    pick = np.zeros((4, 8, 8, 2, 8, 2, 8), np.float32)
    for b in range(8):
        for j in range(8):
            for p in range(2):
                pick[0, b, j, p, b, 0, j] = 1.0
                pick[1, b, j, p, b, 1, j] = 1.0
                pick[2, b, j, p, b, p, j] = 1.0
                pick[3, b, j, p, b, 1 - p, j] = 1.0 - 2.0 * p
    pick = pick.reshape(512, 128)
    made = (forward, inverse, to_modes, to_rows, weave, pick)
    return tuple(np.asarray(t, np.float32).astype(jnp.bfloat16) for t in made)


def mm(a, b):
    return lax.dot_general(a, b, (((1,), (0,)), ((), ())), preferred_element_type=f32)


def mm_nt(a, b):
    return lax.dot_general(a, b, (((1,), (1,)), ((), ())), preferred_element_type=f32)


def mm_tn(a, b):
    return lax.dot_general(a, b, (((0,), (0,)), ((), ())), preferred_element_type=f32)


def low_lanes(shape):
    return lax.broadcasted_iota(jnp.int32, shape, len(shape) - 1) % 128 < HALF


def swap(value):
    return jnp.concatenate([value[:, HALF:], value[:, :HALF]], axis=1)


def spectra_of(table, rows):
    return mm_nt(table, rows).astype(bf16)


def modes_of(received, to_modes):
    both = mm(to_modes, received)
    chosen = jnp.where(low_lanes((128, 128)), both[:128], both[128:])
    return (chosen + swap(chosen)).astype(bf16)


def rows_of(modes, to_rows):
    low = low_lanes((MX, 128))
    turned = swap(modes)
    stacked = jnp.concatenate(
        [
            jnp.where(low, modes, 0.0),
            jnp.where(low, 0.0, turned),
            jnp.where(low, turned, 0.0),
            jnp.where(low, 0.0, modes),
        ],
        axis=0,
    ).astype(bf16)
    return mm(to_rows, stacked).astype(bf16)


def own_block(shape):
    return (
        lax.broadcasted_iota(jnp.int32, shape, 0) % 8
        == lax.broadcasted_iota(jnp.int32, shape, 1) // HALF
    )


def gelu_slope(value):
    return 0.5 * (1.0 + lax.erf(value / math.sqrt(2.0))) + value * jnp.exp(
        -0.5 * value * value
    ) / math.sqrt(2.0 * math.pi)


def spectra_kernel(field_ref, table_ref, weave_ref, out_ref):
    table = table_ref[...]
    parts = [
        spectra_of(table, field_ref[q * 128 : (q + 1) * 128, :]) for q in range(QUAD)
    ]
    out_ref[...] = mm(weave_ref[...], jnp.concatenate(parts, axis=0)).astype(bf16)


def forward_modes_kernel(received_ref, weight_ref, to_modes_ref, to_rows_ref, modes_ref, out_ref):
    modes = modes_of(received_ref[...], to_modes_ref[...])
    modes_ref[...] = modes
    wide = modes.astype(f32)
    own = own_block((16, 512))
    sign = jnp.where(low_lanes((8, 128)), -1.0, 1.0)
    mixed = []
    for block in range(BLOCKS):
        mine = wide[block * 16 : (block + 1) * 16]
        spread = jnp.where(own, jnp.concatenate([mine] * 4, axis=1), 0.0).astype(bf16)
        product = mm(spread, weight_ref[block * 512 : (block + 1) * 512, :])
        mixed.append(product[:8] + sign * swap(product[8:]))
    out_ref[...] = rows_of(jnp.concatenate(mixed, axis=0), to_rows_ref[...])


def backward_modes_kernel(
    received_ref, weight_ref, modes_ref, to_modes_ref, to_rows_ref, pair_ref, out_ref
):
    grads = modes_of(received_ref[...], to_modes_ref[...])
    wide = grads.astype(f32)
    pair_ref[...] = jnp.where(
        low_lanes((128, 128)), modes_ref[...].astype(f32), wide
    ).astype(bf16)
    own = own_block((16, 512))
    low = low_lanes((8, 128))
    mixed = []
    for block in range(BLOCKS):
        real = wide[block * 16 : block * 16 + 8]
        imaginary = wide[block * 16 + 8 : block * 16 + 16]
        turned = jnp.concatenate(
            [jnp.where(low, real, imaginary), jnp.where(low, imaginary, -real)], axis=0
        ).astype(bf16)
        product = mm_nt(turned, weight_ref[block * 512 : (block + 1) * 512, :])
        product = jnp.where(own, product, 0.0)
        folded = product[:, :128] + product[:, 128:256] + product[:, 256:384] + product[:, 384:]
        folded = folded + swap(folded)
        mixed.append(jnp.where(low, folded[:8], folded[8:]))
    out_ref[...] = rows_of(jnp.concatenate(mixed, axis=0), to_rows_ref[...])


def slope_kernel(
    received_ref,
    field_ref,
    cotangent_ref,
    point_ref,
    bias_ref,
    inverse_ref,
    weave_ref,
    grad_ref,
    out_ref,
):
    inverse = inverse_ref[...]
    weave = weave_ref[...]
    rows = mm_tn(weave, received_ref[...]).astype(bf16)
    parts = []
    for q in range(QUAD):
        at = slice(q * 128, (q + 1) * 128)
        value = mm_tn(rows[at], inverse) + mm(point_ref[...], field_ref[at, :]) + bias_ref[...]
        grad = (cotangent_ref[at, :].astype(f32) * gelu_slope(value)).astype(bf16)
        grad_ref[at, :] = grad
        parts.append(spectra_of(inverse, grad))
    out_ref[...] = mm(weave, jnp.concatenate(parts, axis=0)).astype(bf16)


def field_kernel(received_ref, grad_ref, point_ref, forward_ref, weave_ref, out_ref):
    forward = forward_ref[...]
    rows = mm_tn(weave_ref[...], received_ref[...]).astype(bf16)
    for q in range(QUAD):
        at = slice(q * 128, (q + 1) * 128)
        value = mm_tn(rows[at], forward) + mm(point_ref[...], grad_ref[at, :])
        out_ref[at, :] = value.astype(bf16)


def adam_kernel(
    pair_ref, pick_ref, weight_ref, first_ref, second_ref, new_weight_ref, new_first_ref, new_second_ref
):
    width = 512
    bias_one = 1.0 - beta_one**adam_step
    bias_two = 1.0 - beta_two**adam_step
    picked = mm(pick_ref[...], pair_ref[...]).astype(bf16)
    row = lax.broadcasted_iota(jnp.int32, (128, width), 0)
    lane = lax.broadcasted_iota(jnp.int32, (128, width), 1)
    outer = jnp.where(row == HALF + lane % HALF, 1.0, 0.0).astype(bf16)
    right_one = mm(picked[256:384], outer)
    right_two = mm(picked[384:], outer)
    for n in range(C * C // width):
        inner = jnp.where(row == n * (width // HALF) + lane // HALF, 1.0, 0.0).astype(bf16)
        product = mm(picked[:128], inner) * right_one + mm(picked[128:256], inner) * right_two
        gradient = product[:16]
        for b in range(1, 8):
            gradient = gradient + product[b * 16 : (b + 1) * 16]
        at = slice(n * width, (n + 1) * width)
        first = beta_one * first_ref[:, at] + (1.0 - beta_one) * gradient
        second = beta_two * second_ref[:, at] + (1.0 - beta_two) * gradient * gradient
        new_first_ref[:, at] = first
        new_second_ref[:, at] = second
        step = learn_rate * (first / bias_one) / (jnp.sqrt(second / bias_two) + epsilon_adam)
        new_weight_ref[:, at] = weight_ref[:, at] - step


def call(kernel, outs, *arrays):
    return pl.pallas_call(
        kernel,
        out_shape=[jax.ShapeDtypeStruct(shape, dtype) for shape, dtype in outs],
        compiler_params=pltpu.CompilerParams(vmem_limit_bytes=40 * 1024 * 1024),
    )(*arrays)


def exchange(array, axis):
    return lax.all_to_all(array, axis, split_axis=0, concat_axis=0, tiled=True)


def shards(
    in_field, out_grad, point_weight, point_bias, spectral_weight, first_moment, second_moment
):
    forward, inverse, to_modes, to_rows, weave, pick = (jnp.asarray(t) for t in tables())
    field = in_field.reshape(SLAB * C, NY)
    cotangent = out_grad.reshape(SLAB * C, NY)
    zero = jnp.zeros_like(point_weight)
    point = jnp.block([[point_weight, zero], [zero, point_weight]])
    bias = jnp.concatenate([point_bias, point_bias]).reshape(128, 1)
    message = [((512, 128), bf16)]

    (sent,) = call(spectra_kernel, message, field, forward, weave)
    columns = exchange(sent, "grid")

    local = spectral_weight.astype(bf16).reshape(8, 2, C, C).transpose(0, 2, 1, 3).reshape(512, 128)
    whole = exchange(
        jnp.broadcast_to(local[None], (BLOCKS, 512, 128)).reshape(BLOCKS * 512, 128), "dp"
    )

    modes, sent = call(
        forward_modes_kernel, [((128, 128), bf16)] + message, columns, whole, to_modes, to_rows
    )
    received = exchange(sent, "grid")
    pre_grad, sent = call(
        slope_kernel,
        [((512, 512), bf16)] + message,
        received,
        field,
        cotangent,
        point.T,
        bias,
        inverse,
        weave,
    )
    columns = exchange(sent, "grid")
    pair, sent = call(
        backward_modes_kernel,
        [((128, 128), bf16)] + message,
        columns,
        whole,
        modes,
        to_modes,
        to_rows,
    )
    pair = exchange(pair, "dp")
    received = exchange(sent, "grid")
    flat = (16, C * C)
    new_weight, new_first, new_second = call(
        adam_kernel,
        [(flat, f32)] * 3,
        pair,
        pick,
        spectral_weight.reshape(flat),
        first_moment.reshape(flat),
        second_moment.reshape(flat),
    )
    (grad_field,) = call(
        field_kernel, [((512, 512), bf16)], received, pre_grad, point, forward, weave
    )
    shape = spectral_weight.shape
    return (
        grad_field.reshape(in_field.shape),
        new_weight.reshape(shape),
        new_first.reshape(shape),
        new_second.reshape(shape),
    )


def solution(mesh):
    split = P("dp", "grid", None, None)
    return jax.shard_map(
        shards,
        mesh=mesh,
        in_specs=(split, split, P(), P(), split, split, split),
        out_specs=(split, split, split, split),
        check_vma=False,
    )
```

time: 774 us -> 148 us (0.19)
  other arithmetic: 373 us -> 0.25 us
  local copies, waits for them, and re-layouts: 221 us -> 11.7 us
  waiting for transfers between devices: 73.1 us -> 43.4 us
  between operations: 14.9 us -> 0.83 us
  matrix products: 11.4 us -> 0 us
  blocking collectives: 41.9 us -> 52.6 us
  Pallas kernels: 0 us -> 8.99 us
    unnamed x4 -> x0, other arithmetic: 362 us -> none
    unnamed x56 -> x38, local copies, waits for them, and re-layouts: 99.3 us -> 7.46 us
    all_to_all x8 -> x0, local copies, waits for them, and re-layouts: 63 us -> none  [the longest x2 30.7 us: shards(): lax.all_to_all(to_rows(input_modes), 'grid', split_axis=2, concat_axis=1,...]
    reshape x7 -> x9, local copies, waits for them, and re-layouts: 55.4 us -> 3.63 us  [the longest x1 0.85 us: shards(): new_weight.reshape(shape)]
    all_gather x1 -> x0, waiting for transfers between devices: 45.7 us -> none  [shards(): lax.all_gather(local_weight, 'dp', axis=0, tiled=True)]
    all_to_all x2 -> x3, waiting for transfers between devices: 27.4 us -> 43.4 us  [exchange(): return lax.all_to_all(array, axis, split_axis=0, concat_axis=0, tiled=True)]
    dot_general x18 -> x0, matrix products: 11.4 us -> none  [the longest x1 1.43 us: mix_backward(): jnp.einsum('bqko,kqco->bqkc', cotangent[:, :, 0], weight[:, :, 0], prefer...]
    all_to_all x2 -> x3, blocking collectives: 41.9 us -> 52.6 us  [exchange(): return lax.all_to_all(array, axis, split_axis=0, concat_axis=0, tiled=True)]
  transfers between devices with their start and end apart: 4 -> 3, of which waited for: 3 -> 3; matrix products, arithmetic and copies ran while one was open for 38% -> 3% of each run, Pallas kernels for 0% -> 1%
where the time goes in v1:
time: 148 us
  blocking collectives  52.6 us (36%)
  waiting for transfers between devices  43.4 us (29%)
  starting transfers between devices  30 us (20%)
  local copies, waits for them, and re-layouts  11.7 us (8%)
  Pallas kernels  8.99 us (6%)
    all_to_all x3, blocking collectives, exchange(): return lax.all_to_all(array, axis, split_axis=0, concat_axis=0, tiled=True)  52.6 us
    all_to_all x3, waiting for transfers between devices, exchange(): return lax.all_to_all(array, axis, split_axis=0, concat_axis=0, tiled=True)  43.4 us
    all_to_all x3, starting transfers between devices, exchange(): return lax.all_to_all(array, axis, split_axis=0, concat_axis=0, tiled=True)  30 us
    pallas_call x6, Pallas kernels, call(): pl.pallas_call(kernel, out_shape=[jax.ShapeDtypeStruct(shape, dtype) for...  8.99 us
    unnamed x38, local copies, waits for them, and re-layouts  7.46 us
  transfers between devices with their start and end apart: 3, of which 3 were waited for; matrix products, arithmetic and copies ran while one was open for 3% of the time, Pallas kernels for 1%

profile of v1, /device:TPU:1, one launch (start us, length us, event | category | flops | bytes accessed | tf_op | source)
XLA Modules:
  0.0 147.6 jit_solution(7186157630862253586)
XLA Ops:
  0.6 0.0 copy-start
  0.6 1.0 copy-done
  1.7 0.0 copy-start.2
  1.7 1.0 copy-done.2
  2.7 0.0 copy-start.6
  2.7 0.9 copy-done.6
  3.6 1.2 shard_map.156
  4.8 0.0 copy-start.13
  4.8 18.2 %all-to-all-start = ((bf16[64,8,128]{2,1,0:T(8,128)(2,1)}), bf16[64,8,128]{2,1,0:T(8,128)(2,1)S(1)}, u32[]{:S(2)}, u32[]{:S(2)}) async-start(bf16[64,8,128]{2,1,0:T(8,128)(2,1)} %bitcast.1), calls=%async_computation | async-start | bytes 262144 | tf_op jit(solution)/shard_map/all_to_all | solution.py:250
  23.1 0.0 copy-done.13
  23.1 0.1 convert_element_type.3
  23.2 0.2 reshape.57
  23.4 0.2 copy.22
  23.6 0.2 broadcast_in_dim.8
  23.8 0.1 copy.23
  23.9 16.3 %all-to-all-done = bf16[64,8,128]{2,1,0:T(8,128)(2,1)S(1)} async-done(((bf16[64,8,128]{2,1,0:T(8,128)(2,1)}), bf16[64,8,128]{2,1,0:T(8,128)(2,1)S(1)}, u32[]{:S(2)}, u32[]{:S(2)}) %all-to-all-start) | async-done | bytes 131104 | tf_op jit(solution)/shard_map/all_to_all | solution.py:250
  40.2 0.1 broadcast_in_dim.9
  40.3 0.0 copy-start.4
  40.3 0.0 copy-start.5
  40.4 22.6 %all_to_all.63 = bf16[8,512,128]{2,1,0:T(8,128)(2,1)S(1)} all-to-all(bf16[8,512,128]{2,1,0:T(8,128)(2,1)S(1)} %broadcast_in_dim.9), channel_id=1, replica_groups=mesh['grid'=64,'dp'=8] {'dp'}, dimensions={0} | all-to-all | bytes 2097152 | tf_op jit(solution)/shard_map/all_to_all | solution.py:250
  63.0 0.0 copy-done.4
  63.0 0.0 copy-done.5
  63.0 0.0 copy-start.1
  63.0 0.0 copy-start.3
  63.0 1.6 %shard_map.157 = (bf16[128,128]{1,0:T(8,128)(2,1)S(1)}, bf16[512,128]{1,0:T(8,128)(2,1)}) custom-call(bf16[512,128]{1,0:T(8,128)(2,1)S(1)} %bitcast.32, bf16[4096,128]{1,0:T(8,128)(2,1)S(1)} %bitcast.26, bf16[256,512]{1,0:T(8,128)(2,1)S(1)} %copy-done.4, bf16[512,256]{1,0:T(8,128)(2,1)S(1)} %copy-done.5), custom_call_target="tpu_custom_call" | custom-call | tf_op jit(solution)/shard_map/pallas_call | solution.py:242
  64.6 0.0 copy-start.11
  64.6 0.6 copy-done.11
  65.2 0.0 copy-start.17
  65.2 6.0 %all-to-all-start.2 = ((bf16[64,8,128]{2,1,0:T(8,128)(2,1)}), bf16[64,8,128]{2,1,0:T(8,128)(2,1)S(1)}, u32[]{:S(2)}, u32[]{:S(2)}) async-start(bf16[64,8,128]{2,1,0:T(8,128)(2,1)} %bitcast.5), calls=%async_computation.2 | async-start | bytes 262144 | tf_op jit(solution)/shard_map/all_to_all | solution.py:250
  71.2 0.0 copy-done.17
  71.3 0.0 copy-start.10
  71.3 0.1 fusion.2
  71.4 0.1 copy.24.point_ref
  71.5 0.5 copy-done.18
  72.0 0.1 maximum_bitcast_fusion
  72.1 0.1 copy.25.bias_ref
  72.2 16.3 %all-to-all-done.2 = bf16[64,8,128]{2,1,0:T(8,128)(2,1)S(1)} async-done(((bf16[64,8,128]{2,1,0:T(8,128)(2,1)}), bf16[64,8,128]{2,1,0:T(8,128)(2,1)S(1)}, u32[]{:S(2)}, u32[]{:S(2)}) %all-to-all-start.2) | async-done | bytes 131104 | tf_op jit(solution)/shard_map/all_to_all | solution.py:250
  88.5 0.0 copy-done.1
  88.5 0.0 copy-done.3
  88.5 0.0 copy-done.10
  88.5 0.0 copy-start.8
  88.5 1.0 copy-done.8
  89.5 1.8 %shard_map.158 = (bf16[512,512]{1,0:T(8,128)(2,1)S(1)}, bf16[512,128]{1,0:T(8,128)(2,1)S(1)}) custom-call(bf16[512,128]{1,0:T(8,128)(2,1)S(1)} %bitcast.34, bf16[512,512]{1,0:T(8,128)(2,1)S(1)} %bitcast.29, bf16[512,512]{1,0:T(8,128)(2,1)S(1)} %bitcast.31, bf16[128,128]{1,0:T(8,128)(2,1)S(1)} %copy.24.point_ref, f32[128,1]{1,0:T(8,128)S(1)} %copy.25.bias_ref, ...), custom_call_target="tpu_custom_call" | custom-call | tf_op jit(solution)/shard_map/pallas_call | solution.py:242
  91.4 0.0 copy-start.12
  91.4 20.9 %all_to_all.64 = bf16[64,8,128]{2,1,0:T(8,128)(2,1)S(1)} all-to-all(bf16[64,8,128]{2,1,0:T(8,128)(2,1)S(1)} %bitcast.35), channel_id=1, replica_groups=mesh['grid'=64,'dp'=8] {'grid'}, dimensions={0} | all-to-all | bytes 262144 | tf_op jit(solution)/shard_map/all_to_all | solution.py:250
  112.2 0.0 copy-done.12
  112.2 1.6 %shard_map.159 = (bf16[128,128]{1,0:T(8,128)(2,1)S(1)}, bf16[512,128]{1,0:T(8,128)(2,1)}) custom-call(bf16[512,128]{1,0:T(8,128)(2,1)S(1)} %bitcast.33, bf16[4096,128]{1,0:T(8,128)(2,1)S(1)} %bitcast.27, bf16[128,128]{1,0:T(8,128)(2,1)S(1)} %copy-done.12, bf16[256,512]{1,0:T(8,128)(2,1)S(1)} %copy-done.4, bf16[512,256]{1,0:T(8,128)(2,1)S(1)} %copy-done.5), custom_call_target="tpu_custom_call" | custom-call | tf_op jit(solution)/shard_map/pallas_call | solution.py:242
  113.9 9.1 %all_to_all.65 = bf16[8,16,128]{2,1,0:T(8,128)(2,1)S(1)} all-to-all(bf16[8,16,128]{2,1,0:T(8,128)(2,1)S(1)} %bitcast.37), channel_id=1, replica_groups=mesh['grid'=64,'dp'=8] {'dp'}, dimensions={0} | all-to-all | bytes 65536 | tf_op jit(solution)/shard_map/all_to_all | solution.py:250
  123.0 5.8 %all-to-all-start.4 = ((bf16[64,8,128]{2,1,0:T(8,128)(2,1)}), bf16[64,8,128]{2,1,0:T(8,128)(2,1)S(1)}, u32[]{:S(2)}, u32[]{:S(2)}) async-start(bf16[64,8,128]{2,1,0:T(8,128)(2,1)} %bitcast.12), calls=%async_computation.4 | async-start | bytes 262144 | tf_op jit(solution)/shard_map/all_to_all | solution.py:250
  128.7 0.0 copy-done.14
  128.8 0.0 copy-start.15
  128.8 0.2 reshape.61.weight_ref
  129.0 0.8 copy-done.15
  129.7 0.2 reshape.62.first_ref
  129.9 0.8 copy-done.16
  130.7 0.2 reshape.63.second_ref
  130.8 0.7 copy-done.9
  131.6 1.0 shard_map.161
  132.6 0.9 reshape.64
  133.5 0.9 reshape.65
  134.3 0.9 reshape.66
  135.2 10.8 %all-to-all-done.4 = bf16[64,8,128]{2,1,0:T(8,128)(2,1)S(1)} async-done(((bf16[64,8,128]{2,1,0:T(8,128)(2,1)}), bf16[64,8,128]{2,1,0:T(8,128)(2,1)S(1)}, u32[]{:S(2)}, u32[]{:S(2)}) %all-to-all-start.4) | async-done | bytes 131104 | tf_op jit(solution)/shard_map/all_to_all | solution.py:250
  146.0 0.0 copy-done.7
  146.0 1.7 %shard_map.160 = bf16[512,512]{1,0:T(8,128)(2,1)} custom-call(bf16[512,128]{1,0:T(8,128)(2,1)S(1)} %bitcast.30, bf16[512,512]{1,0:T(8,128)(2,1)S(1)} %get-tuple-element.17.grad_ref, bf16[128,128]{1,0:T(8,128)(2,1)S(1)} %get-tuple-element.30.point_ref, bf16[128,512]{1,0:T(8,128)(2,1)S(1)} %copy-done.7, bf16[512,512]{1,0:T(8,128)(2,1)S(1)} %copy-done.1), custom_call_target="tpu_custom_call" | custom-call | tf_op jit(solution)/shard_map/pallas_call | solution.py:242
  (5 shorter events, 0.0 us)
Async XLA Ops:
  0.6 1.0 copy-start
  1.7 1.0 copy-start.2
  2.7 0.9 copy-start.6
  4.8 18.2 %copy-start.13 = (f32[8,1,2,4096]{3,2,1,0:T(2,128)S(1)}, f32[8,1,2,4096]{3,2,1,0:T(2,128)}, u32[]{:S(2)}) copy-start(f32[8,1,2,4096]{3,2,1,0:T(2,128)} %param.17) | copy-start | bytes 786436
  4.8 35.3 %all-to-all-start = ((bf16[64,8,128]{2,1,0:T(8,128)(2,1)}), bf16[64,8,128]{2,1,0:T(8,128)(2,1)S(1)}, u32[]{:S(2)}, u32[]{:S(2)}) async-start(bf16[64,8,128]{2,1,0:T(8,128)(2,1)} %bitcast.1), calls=%async_computation | async-start | bytes 262144 | tf_op jit(solution)/shard_map/all_to_all | solution.py:250
  40.3 22.6 %copy-start.4 = (bf16[256,512]{1,0:T(8,128)(2,1)S(1)}, bf16[256,512]{1,0:T(8,128)(2,1)}, u32[]{:S(2)}) copy-start(bf16[256,512]{1,0:T(8,128)(2,1)} %constant.16.clone.to_modes_ref) | copy-start | bytes 786436
  40.3 22.6 %copy-start.5 = (bf16[512,256]{1,0:T(8,128)(2,1)S(1)}, bf16[512,256]{1,0:T(8,128)(2,1)}, u32[]{:S(2)}) copy-start(bf16[512,256]{1,0:T(8,128)(2,1)} %constant.17.clone.to_rows_ref) | copy-start | bytes 786436
  63.0 25.5 %copy-start.1 = (bf16[512,512]{1,0:T(8,128)(2,1)S(1)}, bf16[512,512]{1,0:T(8,128)(2,1)}, u32[]{:S(2)}) copy-start(bf16[512,512]{1,0:T(8,128)(2,1)} %constant.18.clone.weave_ref) | copy-start | bytes 1572868
  63.0 25.5 %copy-start.3 = (bf16[1,8,64,512]{3,2,1,0:T(8,128)(2,1)S(1)}, bf16[1,8,64,512]{3,2,1,0:T(8,128)(2,1)}, u32[]{:S(2)}) copy-start(bf16[1,8,64,512]{3,2,1,0:T(8,128)(2,1)} %param.13) | copy-start | bytes 1572868
  64.6 0.6 copy-start.11
  65.2 6.0 %copy-start.17 = (bf16[64,64]{1,0:T(8,128)(2,1)S(1)}, bf16[64,64]{1,0:T(8,128)(2,1)}, u32[]{:S(2)}) copy-start(bf16[64,64]{1,0:T(8,128)(2,1)} %param.15) | copy-start | bytes 24580
  65.2 23.3 %all-to-all-start.2 = ((bf16[64,8,128]{2,1,0:T(8,128)(2,1)}), bf16[64,8,128]{2,1,0:T(8,128)(2,1)S(1)}, u32[]{:S(2)}, u32[]{:S(2)}) async-start(bf16[64,8,128]{2,1,0:T(8,128)(2,1)} %bitcast.5), calls=%async_computation.2 | async-start | bytes 262144 | tf_op jit(solution)/shard_map/all_to_all | solution.py:250
  71.3 17.2 %copy-start.10 = (bf16[128,512]{1,0:T(8,128)(2,1)S(1)}, bf16[128,512]{1,0:T(8,128)(2,1)}, u32[]{:S(2)}) copy-start(bf16[128,512]{1,0:T(8,128)(2,1)} %constant.15.clone.inverse_ref) | copy-start | bytes 393220
  71.4 0.7 copy-start.18
  88.5 1.0 copy-start.8
  91.4 20.9 %copy-start.12 = (bf16[128,128]{1,0:T(8,128)(2,1)S(1)}, bf16[128,128]{1,0:T(8,128)(2,1)}, u32[]{:S(2)}) copy-start(bf16[128,128]{1,0:T(8,128)(2,1)} %copy-done.11) | copy-start | bytes 98308
  113.9 14.9 %copy-start.14 = (f32[8,1,2,4096]{3,2,1,0:T(2,128)S(1)}, f32[8,1,2,4096]{3,2,1,0:T(2,128)}, u32[]{:S(2)}) copy-start(f32[8,1,2,4096]{3,2,1,0:T(2,128)} %param.17) | copy-start | bytes 786436
  123.0 23.0 %all-to-all-start.4 = ((bf16[64,8,128]{2,1,0:T(8,128)(2,1)}), bf16[64,8,128]{2,1,0:T(8,128)(2,1)S(1)}, u32[]{:S(2)}, u32[]{:S(2)}) async-start(bf16[64,8,128]{2,1,0:T(8,128)(2,1)} %bitcast.12), calls=%async_computation.4 | async-start | bytes 262144 | tf_op jit(solution)/shard_map/all_to_all | solution.py:250
  128.8 1.0 copy-start.15
  129.7 0.9 copy-start.16
  130.7 0.9 copy-start.9
  134.3 11.7 %copy-start.7 = (bf16[128,512]{1,0:T(8,128)(2,1)S(1)}, bf16[128,512]{1,0:T(8,128)(2,1)}, u32[]{:S(2)}) copy-start(bf16[128,512]{1,0:T(8,128)(2,1)} %constant.14.clone.table_ref.forward_ref) | copy-start | bytes 393220

commit v2 on v1

--- a/solution.py
+++ b/solution.py
@@ -57,8 +57,6 @@
     to_rows = np.stack([np.stack([c, -s], 0), np.stack([s, c], 0)], 0)
     to_rows = to_rows.transpose(3, 0, 4, 1, 5, 2).reshape(512, 256)
 
-    weave = np.eye(512, dtype=np.float32).reshape(QUAD, 128, 512).transpose(1, 0, 2).reshape(512, 512)
-
     pick = np.zeros((4, 8, 8, 2, 8, 2, 8), np.float32)
     for b in range(8):
         for j in range(8):
@@ -68,7 +66,7 @@
                 pick[2, b, j, p, b, p, j] = 1.0
                 pick[3, b, j, p, b, 1 - p, j] = 1.0 - 2.0 * p
     pick = pick.reshape(512, 128)
-    made = (forward, inverse, to_modes, to_rows, weave, pick)
+    made = (forward, inverse, to_modes, to_rows, pick)
     return tuple(np.asarray(t, np.float32).astype(jnp.bfloat16) for t in made)
 
 
@@ -92,8 +90,12 @@
     return jnp.concatenate([value[:, HALF:], value[:, :HALF]], axis=1)
 
 
-def spectra_of(table, rows):
-    return mm_nt(table, rows).astype(bf16)
+def part(q):
+    return slice(q * 128, (q + 1) * 128)
+
+
+def quarter(q):
+    return pl.ds(q, 128, stride=QUAD)
 
 
 def modes_of(received, to_modes):
@@ -130,18 +132,29 @@
     ) / math.sqrt(2.0 * math.pi)
 
 
-def spectra_kernel(field_ref, table_ref, weave_ref, out_ref):
+def spectra_kernel(field_hbm, table_hbm, out_ref, field_ref, table_ref, woven_ref, sems):
+    table_copy = pltpu.make_async_copy(table_hbm, table_ref, sems.at[QUAD])
+    table_copy.start()
+    copies = [
+        pltpu.make_async_copy(field_hbm.at[part(q)], field_ref.at[part(q)], sems.at[q])
+        for q in range(QUAD)
+    ]
+    for copy in copies:
+        copy.start()
+    table_copy.wait()
     table = table_ref[...]
-    parts = [
-        spectra_of(table, field_ref[q * 128 : (q + 1) * 128, :]) for q in range(QUAD)
-    ]
-    out_ref[...] = mm(weave_ref[...], jnp.concatenate(parts, axis=0)).astype(bf16)
-
-
-def forward_modes_kernel(received_ref, weight_ref, to_modes_ref, to_rows_ref, modes_ref, out_ref):
-    modes = modes_of(received_ref[...], to_modes_ref[...])
-    modes_ref[...] = modes
-    wide = modes.astype(f32)
+    for q in range(QUAD):
+        copies[q].wait()
+        woven_ref[quarter(q), :] = mm_nt(table, field_ref[part(q), :])
+    out_ref[...] = woven_ref[...].astype(bf16)
+
+
+def modes_kernel(received_ref, to_modes_ref, modes_ref):
+    modes_ref[...] = modes_of(received_ref[...], to_modes_ref[...])
+
+
+def forward_modes_kernel(modes_ref, weight_ref, to_rows_ref, out_ref):
+    wide = modes_ref[...].astype(f32)
     own = own_block((16, 512))
     sign = jnp.where(low_lanes((8, 128)), -1.0, 1.0)
     mixed = []
@@ -180,35 +193,57 @@
 
 def slope_kernel(
     received_ref,
-    field_ref,
-    cotangent_ref,
+    field_hbm,
+    cotangent_hbm,
     point_ref,
     bias_ref,
     inverse_ref,
-    weave_ref,
     grad_ref,
     out_ref,
-):
+    field_ref,
+    cotangent_ref,
+    woven_ref,
+    sems,
+):
+    copies = []
+    for q in range(QUAD):
+        for n, (source, target) in enumerate(
+            ((field_hbm, field_ref), (cotangent_hbm, cotangent_ref))
+        ):
+            copy = pltpu.make_async_copy(
+                source.at[part(q)], target.at[part(q)], sems.at[2 * q + n]
+            )
+            copy.start()
+            copies.append(copy)
     inverse = inverse_ref[...]
-    weave = weave_ref[...]
-    rows = mm_tn(weave, received_ref[...]).astype(bf16)
-    parts = []
+    woven_ref[...] = received_ref[...].astype(f32)
+    rows = [woven_ref[quarter(q), :].astype(bf16) for q in range(QUAD)]
     for q in range(QUAD):
-        at = slice(q * 128, (q + 1) * 128)
-        value = mm_tn(rows[at], inverse) + mm(point_ref[...], field_ref[at, :]) + bias_ref[...]
-        grad = (cotangent_ref[at, :].astype(f32) * gelu_slope(value)).astype(bf16)
-        grad_ref[at, :] = grad
-        parts.append(spectra_of(inverse, grad))
-    out_ref[...] = mm(weave, jnp.concatenate(parts, axis=0)).astype(bf16)
-
-
-def field_kernel(received_ref, grad_ref, point_ref, forward_ref, weave_ref, out_ref):
+        copies[2 * q].wait()
+        value = mm_tn(rows[q], inverse) + mm(point_ref[...], field_ref[part(q), :])
+        value = value + bias_ref[...]
+        copies[2 * q + 1].wait()
+        grad = (cotangent_ref[part(q), :].astype(f32) * gelu_slope(value)).astype(bf16)
+        grad_ref[part(q), :] = grad
+        woven_ref[quarter(q), :] = mm_nt(inverse, grad)
+    out_ref[...] = woven_ref[...].astype(bf16)
+
+
+def field_kernel(
+    received_ref, grad_ref, point_ref, forward_ref, out_hbm, out_ref, woven_ref, sems
+):
     forward = forward_ref[...]
-    rows = mm_tn(weave_ref[...], received_ref[...]).astype(bf16)
+    woven_ref[...] = received_ref[...].astype(f32)
+    copies = []
     for q in range(QUAD):
-        at = slice(q * 128, (q + 1) * 128)
-        value = mm_tn(rows[at], forward) + mm(point_ref[...], grad_ref[at, :])
-        out_ref[at, :] = value.astype(bf16)
+        rows = woven_ref[quarter(q), :].astype(bf16)
+        value = mm_tn(rows, forward) + mm(point_ref[...], grad_ref[part(q), :])
+        out_ref[part(q), :] = value.astype(bf16)
+        copy = pltpu.make_async_copy(out_ref.at[part(q)], out_hbm.at[part(q)], sems.at[q])
+        copy.start()
+        copies.append(copy)
+    for copy in copies:
+        copy.wait()
 
 
 def adam_kernel(
@@ -238,10 +273,17 @@
         new_weight_ref[:, at] = weight_ref[:, at] - step
 
 
-def call(kernel, outs, *arrays):
+HBM = pl.BlockSpec(memory_space=pl.ANY)
+VMEM = pl.BlockSpec(memory_space=pltpu.VMEM)
+
+
+def call(kernel, outs, *arrays, scratch=(), far=(), far_out=False):
     return pl.pallas_call(
         kernel,
         out_shape=[jax.ShapeDtypeStruct(shape, dtype) for shape, dtype in outs],
+        in_specs=[HBM if n in far else VMEM for n in range(len(arrays))],
+        out_specs=[HBM if far_out else VMEM for _ in outs],
+        scratch_shapes=list(scratch),
         compiler_params=pltpu.CompilerParams(vmem_limit_bytes=40 * 1024 * 1024),
     )(*arrays)
 
@@ -253,7 +295,7 @@
 def shards(
     in_field, out_grad, point_weight, point_bias, spectral_weight, first_moment, second_moment
 ):
-    forward, inverse, to_modes, to_rows, weave, pick = (jnp.asarray(t) for t in tables())
+    forward, inverse, to_modes, to_rows, pick = (jnp.asarray(t) for t in tables())
     field = in_field.reshape(SLAB * C, NY)
     cotangent = out_grad.reshape(SLAB * C, NY)
     zero = jnp.zeros_like(point_weight)
@@ -261,7 +303,18 @@
     bias = jnp.concatenate([point_bias, point_bias]).reshape(128, 1)
     message = [((512, 128), bf16)]
 
-    (sent,) = call(spectra_kernel, message, field, forward, weave)
+    plane = pltpu.VMEM((512, 512), bf16)
+    woven = pltpu.VMEM((512, 128), f32)
+    dma = pltpu.SemaphoreType.DMA
+
+    (sent,) = call(
+        spectra_kernel,
+        message,
+        field,
+        forward,
+        far=(0, 1),
+        scratch=(plane, pltpu.VMEM((128, 512), bf16), woven, dma((QUAD + 1,))),
+    )
     columns = exchange(sent, "grid")
 
     local = spectral_weight.astype(bf16).reshape(8, 2, C, C).transpose(0, 2, 1, 3).reshape(512, 128)
@@ -269,9 +322,8 @@
         jnp.broadcast_to(local[None], (BLOCKS, 512, 128)).reshape(BLOCKS * 512, 128), "dp"
     )
 
-    modes, sent = call(
-        forward_modes_kernel, [((128, 128), bf16)] + message, columns, whole, to_modes, to_rows
-    )
+    (modes,) = call(modes_kernel, [((128, 128), bf16)], columns, to_modes)
+    (sent,) = call(forward_modes_kernel, message, modes, whole, to_rows)
     received = exchange(sent, "grid")
     pre_grad, sent = call(
         slope_kernel,
@@ -282,7 +334,8 @@
         point.T,
         bias,
         inverse,
-        weave,
+        far=(1, 2),
+        scratch=(plane, plane, woven, dma((2 * QUAD,))),
     )
     columns = exchange(sent, "grid")
     pair, sent = call(
@@ -307,7 +360,14 @@
         second_moment.reshape(flat),
     )
     (grad_field,) = call(
-        field_kernel, [((512, 512), bf16)], received, pre_grad, point, forward, weave
+        field_kernel,
+        [((512, 512), bf16)],
+        received,
+        pre_grad,
+        point,
+        forward,
+        far_out=True,
+        scratch=(plane, woven, dma((QUAD,))),
     )
     shape = spectral_weight.shape
     return (

time: 148 us -> 149 us (level)
  blocking collectives: 52.6 us -> 30 us
  waiting for transfers between devices: 43.4 us -> 59.1 us
  starting transfers between devices: 30 us -> 36.2 us
  Pallas kernels: 8.99 us -> 11.3 us
  local copies, waits for them, and re-layouts: 11.7 us -> 9.97 us
    all_to_all x3 -> x2, blocking collectives: 52.6 us -> 30 us  [exchange(): return lax.all_to_all(array, axis, split_axis=0, concat_axis=0, tiled=True)]
    all_to_all x3 -> x4, waiting for transfers between devices: 43.4 us -> 59.1 us  [exchange(): return lax.all_to_all(array, axis, split_axis=0, concat_axis=0, tiled=True)]
    all_to_all x3 -> x4, starting transfers between devices: 30 us -> 36.2 us  [exchange(): return lax.all_to_all(array, axis, split_axis=0, concat_axis=0, tiled=True)]
    unnamed x38 -> x32, local copies, waits for them, and re-layouts: 7.46 us -> 4.77 us
    pallas_call x6 -> x7, Pallas kernels: 8.99 us -> 11.3 us  [call(): pl.pallas_call(kernel, out_shape=[jax.ShapeDtypeStruct(shape, dtype) for...]
  transfers between devices with their start and end apart: 3 -> 4, of which waited for: 3 -> 4; matrix products, arithmetic and copies ran while one was open for 3% -> 3% of each run, Pallas kernels for 1% -> 1%
where the time goes in v2:
time: 149 us; the launch traced here: 148 us
  waiting for transfers between devices  59.1 us (40%)
  starting transfers between devices  36.2 us (24%)
  blocking collectives  30 us (20%)
  Pallas kernels  11.3 us (8%)
  local copies, waits for them, and re-layouts  9.97 us (7%)
    all_to_all x4, waiting for transfers between devices, exchange(): return lax.all_to_all(array, axis, split_axis=0, concat_axis=0, tiled=True)  59.1 us
    all_to_all x4, starting transfers between devices, exchange(): return lax.all_to_all(array, axis, split_axis=0, concat_axis=0, tiled=True)  36.2 us
    all_to_all x2, blocking collectives, exchange(): return lax.all_to_all(array, axis, split_axis=0, concat_axis=0, tiled=True)  30 us
    pallas_call x7, Pallas kernels, call(): pl.pallas_call(kernel, out_shape=[jax.ShapeDtypeStruct(shape, dtype) for...  11.3 us
    unnamed x32, local copies, waits for them, and re-layouts  4.77 us
  transfers between devices with their start and end apart: 4, of which 4 were waited for; matrix products, arithmetic and copies ran while one was open for 3% of the time, Pallas kernels for 1%

profile of v2, /device:TPU:1, one launch (start us, length us, event | category | flops | bytes accessed | tf_op | source)
XLA Modules:
  0.0 148.2 jit_solution(1823164116463761552)
XLA Ops:
  0.6 0.0 copy-start
  0.6 1.0 copy-done
  1.7 0.9 copy-done.5
  2.6 2.4 %shard_map.147 = bf16[512,128]{1,0:T(8,128)(2,1)} custom-call(bf16[512,512]{1,0:T(8,128)(2,1)S(1)} %bitcast.28, bf16[128,512]{1,0:T(8,128)(2,1)S(1)} %copy-done.5), custom_call_target="tpu_custom_call" | custom-call | tf_op jit(solution)/shard_map/pallas_call | solution.py:281
  5.0 0.0 copy-start.10
  5.0 18.2 %all-to-all-start = ((bf16[64,8,128]{2,1,0:T(8,128)(2,1)}), bf16[64,8,128]{2,1,0:T(8,128)(2,1)S(1)}, u32[]{:S(2)}, u32[]{:S(2)}) async-start(bf16[64,8,128]{2,1,0:T(8,128)(2,1)} %bitcast.1), calls=%async_computation | async-start | bytes 262144 | tf_op jit(solution)/shard_map/all_to_all | solution.py:292
  23.2 0.0 copy-done.10
  23.2 0.1 convert_element_type.3
  23.3 0.2 reshape.57
  23.6 0.2 copy.21
  23.8 0.2 broadcast_in_dim.8
  24.0 0.1 copy.22
  24.1 16.3 %all-to-all-done = bf16[64,8,128]{2,1,0:T(8,128)(2,1)S(1)} async-done(((bf16[64,8,128]{2,1,0:T(8,128)(2,1)}), bf16[64,8,128]{2,1,0:T(8,128)(2,1)S(1)}, u32[]{:S(2)}, u32[]{:S(2)}) %all-to-all-start) | async-done | bytes 131104 | tf_op jit(solution)/shard_map/all_to_all | solution.py:292
  40.4 1.1 broadcast_in_dim.9
  41.5 0.0 copy-start.2
  41.5 6.5 %all-to-all-start.1 = ((bf16[8,512,128]{2,1,0:T(8,128)(2,1)}), bf16[8,512,128]{2,1,0:T(8,128)(2,1)S(1)}, u32[]{:S(2)}, u32[]{:S(2)}) async-start(bf16[8,512,128]{2,1,0:T(8,128)(2,1)} %broadcast_in_dim.9), calls=%async_computation.1 | async-start | bytes 2097152 | tf_op jit(solution)/shard_map/all_to_all | solution.py:292
  48.0 0.0 copy-start.3
  48.0 0.0 copy-done.2
  48.0 0.3 shard_map.148.modes_ref
  48.3 16.3 %all-to-all-done.1 = bf16[8,512,128]{2,1,0:T(8,128)(2,1)S(1)} async-done(((bf16[8,512,128]{2,1,0:T(8,128)(2,1)}), bf16[8,512,128]{2,1,0:T(8,128)(2,1)S(1)}, u32[]{:S(2)}, u32[]{:S(2)}) %all-to-all-start.1) | async-done | bytes 1048608 | tf_op jit(solution)/shard_map/all_to_all | solution.py:292
  64.6 0.0 copy-done.3
  64.6 0.0 copy-start.1
  64.6 0.0 copy-start.4
  64.6 1.3 shard_map.149
  65.9 0.0 copy-start.14
  65.9 5.8 %all-to-all-start.2 = ((bf16[64,8,128]{2,1,0:T(8,128)(2,1)}), bf16[64,8,128]{2,1,0:T(8,128)(2,1)S(1)}, u32[]{:S(2)}, u32[]{:S(2)}) async-start(bf16[64,8,128]{2,1,0:T(8,128)(2,1)} %bitcast.5), calls=%async_computation.2 | async-start | bytes 262144 | tf_op jit(solution)/shard_map/all_to_all | solution.py:292
  71.7 0.0 copy-done.14
  71.7 0.0 copy-start.8
  71.7 0.7 fusion.2
  72.4 0.0 copy-start.15
  72.4 0.1 copy.23.point_ref
  72.5 0.5 copy-done.15
  73.0 0.1 maximum_bitcast_fusion
  73.1 0.1 copy.24.bias_ref
  73.2 15.7 %all-to-all-done.2 = bf16[64,8,128]{2,1,0:T(8,128)(2,1)S(1)} async-done(((bf16[64,8,128]{2,1,0:T(8,128)(2,1)}), bf16[64,8,128]{2,1,0:T(8,128)(2,1)S(1)}, u32[]{:S(2)}, u32[]{:S(2)}) %all-to-all-start.2) | async-done | bytes 131104 | tf_op jit(solution)/shard_map/all_to_all | solution.py:292
  88.9 0.0 copy-done.1
  88.9 0.0 copy-done.4
  88.9 0.0 copy-done.8
  88.9 3.6 %shard_map.150 = (bf16[512,512]{1,0:T(8,128)(2,1)S(1)}, bf16[512,128]{1,0:T(8,128)(2,1)S(1)}) custom-call(bf16[512,128]{1,0:T(8,128)(2,1)S(1)} %bitcast.33, bf16[512,512]{1,0:T(8,128)(2,1)S(1)} %bitcast.29, bf16[512,512]{1,0:T(8,128)(2,1)S(1)} %bitcast.31, bf16[128,128]{1,0:T(8,128)(2,1)S(1)} %copy.23.point_ref, f32[128,1]{1,0:T(8,128)S(1)} %copy.24.bias_ref, ...), custom_call_target="tpu_custom_call" | custom-call | tf_op jit(solution)/shard_map/pallas_call | solution.py:281
  92.5 20.9 %all_to_all.63 = bf16[64,8,128]{2,1,0:T(8,128)(2,1)S(1)} all-to-all(bf16[64,8,128]{2,1,0:T(8,128)(2,1)S(1)} %bitcast.35), channel_id=1, replica_groups=mesh['grid'=64,'dp'=8] {'grid'}, dimensions={0} | all-to-all | bytes 262144 | tf_op jit(solution)/shard_map/all_to_all | solution.py:292
  113.3 1.6 %shard_map.151 = (bf16[128,128]{1,0:T(8,128)(2,1)S(1)}, bf16[512,128]{1,0:T(8,128)(2,1)}) custom-call(bf16[512,128]{1,0:T(8,128)(2,1)S(1)} %bitcast.34, bf16[4096,128]{1,0:T(8,128)(2,1)S(1)} %bitcast.27, bf16[128,128]{1,0:T(8,128)(2,1)S(1)} %shard_map.148.modes_ref, bf16[256,512]{1,0:T(8,128)(2,1)S(1)} %copy-done.2, bf16[512,256]{1,0:T(8,128)(2,1)S(1)} %copy-done.3), custom_call_target="tpu_custom_call" | custom-call | tf_op jit(solution)/shard_map/pallas_call | solution.py:281
  115.0 0.0 copy-start.11
  115.0 9.1 %all_to_all.64 = bf16[8,16,128]{2,1,0:T(8,128)(2,1)S(1)} all-to-all(bf16[8,16,128]{2,1,0:T(8,128)(2,1)S(1)} %bitcast.37), channel_id=1, replica_groups=mesh['grid'=64,'dp'=8] {'dp'}, dimensions={0} | all-to-all | bytes 65536 | tf_op jit(solution)/shard_map/all_to_all | solution.py:292
  124.1 5.7 %all-to-all-start.4 = ((bf16[64,8,128]{2,1,0:T(8,128)(2,1)}), bf16[64,8,128]{2,1,0:T(8,128)(2,1)S(1)}, u32[]{:S(2)}, u32[]{:S(2)}) async-start(bf16[64,8,128]{2,1,0:T(8,128)(2,1)} %bitcast.12), calls=%async_computation.4 | async-start | bytes 262144 | tf_op jit(solution)/shard_map/all_to_all | solution.py:292
  129.8 0.0 copy-done.11
  129.8 0.0 copy-start.12
  129.8 0.2 reshape.61.weight_ref
  130.0 0.8 copy-done.12
  130.8 0.0 copy-start.13
  130.8 0.2 reshape.62.first_ref
  131.0 0.8 copy-done.13
  131.7 0.0 copy-start.7
  131.7 0.2 reshape.63.second_ref
  131.9 0.7 copy-done.7
  132.6 1.0 shard_map.153
  133.7 0.9 reshape.64
  134.5 0.9 reshape.65
  135.4 0.0 copy-start.6
  135.4 0.0 copy-start.9
  135.4 0.9 reshape.66
  136.2 10.8 %all-to-all-done.4 = bf16[64,8,128]{2,1,0:T(8,128)(2,1)S(1)} async-done(((bf16[64,8,128]{2,1,0:T(8,128)(2,1)}), bf16[64,8,128]{2,1,0:T(8,128)(2,1)S(1)}, u32[]{:S(2)}, u32[]{:S(2)}) %all-to-all-start.4) | async-done | bytes 131104 | tf_op jit(solution)/shard_map/all_to_all | solution.py:292
  147.0 0.0 copy-done.6
  147.0 0.0 copy-done.9
  147.0 1.1 shard_map.152
  (1 shorter events, 0.0 us)
Async XLA Ops:
  0.6 1.0 copy-start
  1.7 0.9 copy-start.5
  5.0 18.2 %copy-start.10 = (f32[8,1,2,4096]{3,2,1,0:T(2,128)S(1)}, f32[8,1,2,4096]{3,2,1,0:T(2,128)}, u32[]{:S(2)}) copy-start(f32[8,1,2,4096]{3,2,1,0:T(2,128)} %param.16) | copy-start | bytes 786436
  5.0 35.4 %all-to-all-start = ((bf16[64,8,128]{2,1,0:T(8,128)(2,1)}), bf16[64,8,128]{2,1,0:T(8,128)(2,1)S(1)}, u32[]{:S(2)}, u32[]{:S(2)}) async-start(bf16[64,8,128]{2,1,0:T(8,128)(2,1)} %bitcast.1), calls=%async_computation | async-start | bytes 262144 | tf_op jit(solution)/shard_map/all_to_all | solution.py:292
  41.5 6.5 %copy-start.2 = (bf16[256,512]{1,0:T(8,128)(2,1)S(1)}, bf16[256,512]{1,0:T(8,128)(2,1)}, u32[]{:S(2)}) copy-start(bf16[256,512]{1,0:T(8,128)(2,1)} %constant.14.clone.to_modes_ref) | copy-start | bytes 786436
  41.5 23.1 %all-to-all-start.1 = ((bf16[8,512,128]{2,1,0:T(8,128)(2,1)}), bf16[8,512,128]{2,1,0:T(8,128)(2,1)S(1)}, u32[]{:S(2)}, u32[]{:S(2)}) async-start(bf16[8,512,128]{2,1,0:T(8,128)(2,1)} %broadcast_in_dim.9), calls=%async_computation.1 | async-start | bytes 2097152 | tf_op jit(solution)/shard_map/all_to_all | solution.py:292
  48.0 16.6 %copy-start.3 = (bf16[512,256]{1,0:T(8,128)(2,1)S(1)}, bf16[512,256]{1,0:T(8,128)(2,1)}, u32[]{:S(2)}) copy-start(bf16[512,256]{1,0:T(8,128)(2,1)} %constant.15.clone.to_rows_ref) | copy-start | bytes 786436
  64.6 24.3 %copy-start.1 = (bf16[1,8,64,512]{3,2,1,0:T(8,128)(2,1)S(1)}, bf16[1,8,64,512]{3,2,1,0:T(8,128)(2,1)}, u32[]{:S(2)}) copy-start(bf16[1,8,64,512]{3,2,1,0:T(8,128)(2,1)} %param.12) | copy-start | bytes 1572868
  64.6 24.3 %copy-start.4 = (bf16[1,8,64,512]{3,2,1,0:T(8,128)(2,1)S(1)}, bf16[1,8,64,512]{3,2,1,0:T(8,128)(2,1)}, u32[]{:S(2)}) copy-start(bf16[1,8,64,512]{3,2,1,0:T(8,128)(2,1)} %param.13) | copy-start | bytes 1572868
  65.9 5.8 %copy-start.14 = (bf16[64,64]{1,0:T(8,128)(2,1)S(1)}, bf16[64,64]{1,0:T(8,128)(2,1)}, u32[]{:S(2)}) copy-start(bf16[64,64]{1,0:T(8,128)(2,1)} %param.14) | copy-start | bytes 24580
  65.9 23.0 %all-to-all-start.2 = ((bf16[64,8,128]{2,1,0:T(8,128)(2,1)}), bf16[64,8,128]{2,1,0:T(8,128)(2,1)S(1)}, u32[]{:S(2)}, u32[]{:S(2)}) async-start(bf16[64,8,128]{2,1,0:T(8,128)(2,1)} %bitcast.5), calls=%async_computation.2 | async-start | bytes 262144 | tf_op jit(solution)/shard_map/all_to_all | solution.py:292
  71.7 17.2 %copy-start.8 = (bf16[128,512]{1,0:T(8,128)(2,1)S(1)}, bf16[128,512]{1,0:T(8,128)(2,1)}, u32[]{:S(2)}) copy-start(bf16[128,512]{1,0:T(8,128)(2,1)} %constant.13.clone.inverse_ref) | copy-start | bytes 393220
  72.4 0.7 copy-start.15
  115.0 14.8 %copy-start.11 = (f32[8,1,2,4096]{3,2,1,0:T(2,128)S(1)}, f32[8,1,2,4096]{3,2,1,0:T(2,128)}, u32[]{:S(2)}) copy-start(f32[8,1,2,4096]{3,2,1,0:T(2,128)} %param.16) | copy-start | bytes 786436
  124.1 23.0 %all-to-all-start.4 = ((bf16[64,8,128]{2,1,0:T(8,128)(2,1)}), bf16[64,8,128]{2,1,0:T(8,128)(2,1)S(1)}, u32[]{:S(2)}, u32[]{:S(2)}) async-start(bf16[64,8,128]{2,1,0:T(8,128)(2,1)} %bitcast.12), calls=%async_computation.4 | async-start | bytes 262144 | tf_op jit(solution)/shard_map/all_to_all | solution.py:292
  129.8 1.0 copy-start.12
  130.8 0.9 copy-start.13
  131.7 0.9 copy-start.7
  135.4 11.7 %copy-start.6 = (bf16[128,512]{1,0:T(8,128)(2,1)S(1)}, bf16[128,512]{1,0:T(8,128)(2,1)}, u32[]{:S(2)}) copy-start(bf16[128,512]{1,0:T(8,128)(2,1)} %constant.12.clone.table_hbm.forward_ref) | copy-start | bytes 393220
  135.4 11.7 %copy-start.9 = (bf16[128,128]{1,0:T(8,128)(2,1)S(1)}, bf16[128,128]{1,0:T(8,128)(2,1)}, u32[]{:S(2)}) copy-start(bf16[128,128]{1,0:T(8,128)(2,1)} %get-tuple-element.26.point_ref) | copy-start | bytes 98308

commit v3 on v2

--- a/solution.py
+++ b/solution.py
@@ -147,6 +147,11 @@
         copies[q].wait()
         woven_ref[quarter(q), :] = mm_nt(table, field_ref[part(q), :])
     out_ref[...] = woven_ref[...].astype(bf16)
+
+
+def copies_kernel(local_ref, out_ref):
+    for block in range(BLOCKS):
+        out_ref[block * 512 : (block + 1) * 512, :] = local_ref[...]
 
 
 def modes_kernel(received_ref, to_modes_ref, modes_ref):
@@ -191,38 +196,22 @@
     out_ref[...] = rows_of(jnp.concatenate(mixed, axis=0), to_rows_ref[...])
 
 
+def linear_kernel(field_ref, cotangent_hbm, point_ref, bias_ref, out_ref, cotangent_ref, sems):
+    copy = pltpu.make_async_copy(cotangent_hbm, cotangent_ref, sems.at[0])
+    copy.start()
+    for q in range(QUAD):
+        out_ref[part(q), :] = mm(point_ref[...], field_ref[part(q), :]) + bias_ref[...]
+    copy.wait()
+
+
 def slope_kernel(
-    received_ref,
-    field_hbm,
-    cotangent_hbm,
-    point_ref,
-    bias_ref,
-    inverse_ref,
-    grad_ref,
-    out_ref,
-    field_ref,
-    cotangent_ref,
-    woven_ref,
-    sems,
+    received_ref, linear_ref, cotangent_ref, inverse_ref, grad_ref, out_ref, woven_ref
 ):
-    copies = []
-    for q in range(QUAD):
-        for n, (source, target) in enumerate(
-            ((field_hbm, field_ref), (cotangent_hbm, cotangent_ref))
-        ):
-            copy = pltpu.make_async_copy(
-                source.at[part(q)], target.at[part(q)], sems.at[2 * q + n]
-            )
-            copy.start()
-            copies.append(copy)
     inverse = inverse_ref[...]
     woven_ref[...] = received_ref[...].astype(f32)
     rows = [woven_ref[quarter(q), :].astype(bf16) for q in range(QUAD)]
     for q in range(QUAD):
-        copies[2 * q].wait()
-        value = mm_tn(rows[q], inverse) + mm(point_ref[...], field_ref[part(q), :])
-        value = value + bias_ref[...]
-        copies[2 * q + 1].wait()
+        value = mm_tn(rows[q], inverse) + linear_ref[part(q), :]
         grad = (cotangent_ref[part(q), :].astype(f32) * gelu_slope(value)).astype(bf16)
         grad_ref[part(q), :] = grad
         woven_ref[quarter(q), :] = mm_nt(inverse, grad)
@@ -230,8 +219,27 @@
 
 
 def field_kernel(
-    received_ref, grad_ref, point_ref, forward_ref, out_hbm, out_ref, woven_ref, sems
+    received_ref,
+    grad_ref,
+    point_ref,
+    forward_ref,
+    weight_hbm,
+    first_hbm,
+    second_hbm,
+    out_hbm,
+    weight_out,
+    first_out,
+    second_out,
+    out_ref,
+    woven_ref,
+    masters_ref,
+    sems,
 ):
+    loads = []
+    for n, source in enumerate((weight_hbm, first_hbm, second_hbm)):
+        copy = pltpu.make_async_copy(source, masters_ref.at[n], sems.at[QUAD + n])
+        copy.start()
+        loads.append(copy)
     forward = forward_ref[...]
     woven_ref[...] = received_ref[...].astype(f32)
     copies = []
@@ -242,6 +250,10 @@
         copy = pltpu.make_async_copy(out_ref.at[part(q)], out_hbm.at[part(q)], sems.at[q])
         copy.start()
         copies.append(copy)
+    for n, target in enumerate((weight_out, first_out, second_out)):
+        loads[n].wait()
+        for j in range(8):
+            target[2 * j : 2 * j + 2, :] = masters_ref[n, j, 0]
     for copy in copies:
         copy.wait()
 
@@ -267,24 +279,32 @@
         at = slice(n * width, (n + 1) * width)
         first = beta_one * first_ref[:, at] + (1.0 - beta_one) * gradient
         second = beta_two * second_ref[:, at] + (1.0 - beta_two) * gradient * gradient
-        new_first_ref[:, at] = first
-        new_second_ref[:, at] = second
         step = learn_rate * (first / bias_one) / (jnp.sqrt(second / bias_two) + epsilon_adam)
-        new_weight_ref[:, at] = weight_ref[:, at] - step
-
-
-HBM = pl.BlockSpec(memory_space=pl.ANY)
+        weight = weight_ref[:, at] - step
+        for j in range(8):
+            rows = slice(2 * j, 2 * j + 2)
+            new_weight_ref[j, 0, :, at] = weight[rows]
+            new_first_ref[j, 0, :, at] = first[rows]
+            new_second_ref[j, 0, :, at] = second[rows]
+
+
+HBM = pl.BlockSpec(memory_space=pltpu.HBM)
 VMEM = pl.BlockSpec(memory_space=pltpu.VMEM)
 
 
-def call(kernel, outs, *arrays, scratch=(), far=(), far_out=False):
+def call(kernel, outs, *arrays, scratch=(), far=(), far_out=(), near_out=False):
+    arrays = [
+        pltpu.with_memory_space_constraint(a, pltpu.HBM) if n in far else a
+        for n, a in enumerate(arrays)
+    ]
+    place = pltpu.VMEM if near_out else jax.ShapeDtypeStruct
     return pl.pallas_call(
         kernel,
-        out_shape=[jax.ShapeDtypeStruct(shape, dtype) for shape, dtype in outs],
+        out_shape=[place(shape, dtype) for shape, dtype in outs],
         in_specs=[HBM if n in far else VMEM for n in range(len(arrays))],
-        out_specs=[HBM if far_out else VMEM for _ in outs],
+        out_specs=[HBM if n in far_out else VMEM for n in range(len(outs))],
         scratch_shapes=list(scratch),
-        compiler_params=pltpu.CompilerParams(vmem_limit_bytes=40 * 1024 * 1024),
+        compiler_params=pltpu.CompilerParams(vmem_limit_bytes=24 * 1024 * 1024),
     )(*arrays)
 
 
@@ -318,24 +338,32 @@
     columns = exchange(sent, "grid")
 
     local = spectral_weight.astype(bf16).reshape(8, 2, C, C).transpose(0, 2, 1, 3).reshape(512, 128)
-    whole = exchange(
-        jnp.broadcast_to(local[None], (BLOCKS, 512, 128)).reshape(BLOCKS * 512, 128), "dp"
-    )
+    (copies,) = call(copies_kernel, [((BLOCKS * 512, 128), bf16)], local, near_out=True)
+    whole = exchange(copies, "dp")
 
     (modes,) = call(modes_kernel, [((128, 128), bf16)], columns, to_modes)
+    linear, near = call(
+        linear_kernel,
+        [((512, 512), f32), ((512, 512), bf16)],
+        field,
+        cotangent,
+        point.T,
+        bias,
+        far=(1,),
+        scratch=(dma((1,)),),
+        near_out=True,
+    )
+    modes, linear, near = lax.optimization_barrier((modes, linear, near))
     (sent,) = call(forward_modes_kernel, message, modes, whole, to_rows)
     received = exchange(sent, "grid")
     pre_grad, sent = call(
         slope_kernel,
         [((512, 512), bf16)] + message,
         received,
-        field,
-        cotangent,
-        point.T,
-        bias,
+        linear,
+        near,
         inverse,
-        far=(1, 2),
-        scratch=(plane, plane, woven, dma((2 * QUAD,))),
+        scratch=(woven,),
     )
     columns = exchange(sent, "grid")
     pair, sent = call(
@@ -347,35 +375,24 @@
         to_modes,
         to_rows,
     )
+    received, pair = lax.optimization_barrier((exchange(sent, "grid"), pair))
     pair = exchange(pair, "dp")
-    received = exchange(sent, "grid")
-    flat = (16, C * C)
-    new_weight, new_first, new_second = call(
-        adam_kernel,
-        [(flat, f32)] * 3,
-        pair,
-        pick,
-        spectral_weight.reshape(flat),
-        first_moment.reshape(flat),
-        second_moment.reshape(flat),
-    )
-    (grad_field,) = call(
+    masters = (spectral_weight, first_moment, second_moment)
+    shape = spectral_weight.shape
+    grad_field, *flat = call(
         field_kernel,
-        [((512, 512), bf16)],
+        [((512, 512), bf16)] + [((16, C * C), f32)] * 3,
         received,
         pre_grad,
         point,
         forward,
-        far_out=True,
-        scratch=(plane, woven, dma((QUAD,))),
-    )
-    shape = spectral_weight.shape
-    return (
-        grad_field.reshape(in_field.shape),
-        new_weight.reshape(shape),
-        new_first.reshape(shape),
-        new_second.reshape(shape),
-    )
+        *masters,
+        far=(4, 5, 6),
+        far_out=(0,),
+        scratch=(plane, woven, pltpu.VMEM((3,) + shape, f32), dma((QUAD + 3,))),
+    )
+    new_weight, new_first, new_second = call(adam_kernel, [(shape, f32)] * 3, pair, pick, *flat)
+    return (grad_field.reshape(in_field.shape), new_weight, new_first, new_second)
 
 
 def solution(mesh):

time: 149 us -> 141 us (0.946)
  blocking collectives: 30 us -> 64 us
  waiting for transfers between devices: 59.1 us -> 33.8 us
  starting transfers between devices: 36.2 us -> 28.1 us
  local copies, waits for them, and re-layouts: 9.97 us -> 2.29 us
    all_to_all x2 -> x3, blocking collectives: 30 us -> 64 us  [exchange(): return lax.all_to_all(array, axis, split_axis=0, concat_axis=0, tiled=True)]
    all_to_all x4 -> x3, waiting for transfers between devices: 59.1 us -> 33.8 us  [exchange(): return lax.all_to_all(array, axis, split_axis=0, concat_axis=0, tiled=True)]
    all_to_all x4 -> x3, starting transfers between devices: 36.2 us -> 28.1 us  [exchange(): return lax.all_to_all(array, axis, split_axis=0, concat_axis=0, tiled=True)]
    unnamed x32 -> x22, local copies, waits for them, and re-layouts: 4.77 us -> 1.44 us
    reshape x6 -> x0, local copies, waits for them, and re-layouts: 3.1 us -> none  [the longest x1 0.85 us: shards(): new_weight.reshape(shape)]
    pallas_call x7 -> x9, Pallas kernels: 11.3 us -> 11 us  [call(): pl.pallas_call(kernel, out_shape=[place(shape, dtype) for shape, dtype in...]
  transfers between devices with their start and end apart: 4 -> 3, of which waited for: 4 -> 3; matrix products, arithmetic and copies ran while one was open for 3% -> 1% of each run, Pallas kernels for 1% -> 3%
where the time goes in v3:
time: 141 us; the launch traced here: 140 us
  blocking collectives  64 us (45%)
  waiting for transfers between devices  33.8 us (24%)
  starting transfers between devices  28.1 us (20%)
  Pallas kernels  11 us (8%)
  local copies, waits for them, and re-layouts  2.29 us (2%)
    all_to_all x3, blocking collectives, exchange(): return lax.all_to_all(array, axis, split_axis=0, concat_axis=0, tiled=True)  64 us
    all_to_all x3, waiting for transfers between devices, exchange(): return lax.all_to_all(array, axis, split_axis=0, concat_axis=0, tiled=True)  33.8 us
    all_to_all x3, starting transfers between devices, exchange(): return lax.all_to_all(array, axis, split_axis=0, concat_axis=0, tiled=True)  28.1 us
    pallas_call x9, Pallas kernels, call(): pl.pallas_call(kernel, out_shape=[place(shape, dtype) for shape, dtype in...  11 us
  transfers between devices with their start and end apart: 3, of which 3 were waited for; matrix products, arithmetic and copies ran while one was open for 1% of the time, Pallas kernels for 3%

profile of v3, /device:TPU:1, one launch (start us, length us, event | category | flops | bytes accessed | tf_op | source)
XLA Modules:
  0.0 140.2 jit_solution(6669880898658578939)
XLA Ops:
  0.6 2.6 %shard_map.147 = bf16[512,128]{1,0:T(8,128)(2,1)} custom-call(bf16[512,512]{1,0:T(8,128)(2,1)} %bitcast.24, bf16[128,512]{1,0:T(8,128)(2,1)} %constant.12.clone.table_hbm.forward_ref), custom_call_target="tpu_custom_call" | custom-call | tf_op jit(solution)/shard_map/pallas_call | solution.py:301
  3.2 0.0 copy-start.8
  3.2 18.2 %all-to-all-start = ((bf16[64,8,128]{2,1,0:T(8,128)(2,1)}), bf16[64,8,128]{2,1,0:T(8,128)(2,1)S(1)}, u32[]{:S(2)}, u32[]{:S(2)}) async-start(bf16[64,8,128]{2,1,0:T(8,128)(2,1)} %bitcast.1), calls=%async_computation | async-start | bytes 262144 | tf_op jit(solution)/shard_map/all_to_all | solution.py:312
  21.4 0.0 copy-done.8
  21.4 0.1 convert_element_type.3
  21.5 0.2 reshape.41
  21.8 0.3 copy.20
  22.0 0.1 reshape.42.local_ref
  22.2 1.1 shard_map.150
  23.3 15.2 %all-to-all-done = bf16[64,8,128]{2,1,0:T(8,128)(2,1)S(1)} async-done(((bf16[64,8,128]{2,1,0:T(8,128)(2,1)}), bf16[64,8,128]{2,1,0:T(8,128)(2,1)S(1)}, u32[]{:S(2)}, u32[]{:S(2)}) %all-to-all-start) | async-done | bytes 131104 | tf_op jit(solution)/shard_map/all_to_all | solution.py:312
  38.6 0.0 copy-start.10
  38.6 0.0 copy-start
  38.6 6.5 %all-to-all-start.1 = ((bf16[8,512,128]{2,1,0:T(8,128)(2,1)}), bf16[8,512,128]{2,1,0:T(8,128)(2,1)S(1)}, u32[]{:S(2)}, u32[]{:S(2)}) async-start(bf16[8,512,128]{2,1,0:T(8,128)(2,1)} %bitcast.7), calls=%async_computation.1 | async-start | bytes 2097152 | tf_op jit(solution)/shard_map/all_to_all | solution.py:312
  45.0 0.0 copy-done.10
  45.1 0.1 maximum_bitcast_fusion
  45.1 0.0 copy-start.9
  45.1 0.1 copy.17.bias_ref
  45.2 0.6 copy-done.9
  45.8 0.1 fusion.2
  45.9 0.1 copy.16.point_ref
  46.0 0.0 copy-done
  46.1 0.0 copy-start.1
  46.1 1.1 shard_map.149
  47.2 0.0 copy-start.3
  47.2 0.8 copy-done.3
  48.0 0.0 copy-start.2
  48.0 0.0 copy-done.1
  48.0 0.3 shard_map.148.modes_ref
  48.3 13.4 %all-to-all-done.1 = bf16[8,512,128]{2,1,0:T(8,128)(2,1)S(1)} async-done(((bf16[8,512,128]{2,1,0:T(8,128)(2,1)}), bf16[8,512,128]{2,1,0:T(8,128)(2,1)S(1)}, u32[]{:S(2)}, u32[]{:S(2)}) %all-to-all-start.1) | async-done | bytes 1048608 | tf_op jit(solution)/shard_map/all_to_all | solution.py:312
  61.7 0.0 copy-done.2
  61.7 0.0 copy-start.4
  61.7 0.6 shard_map.151
  62.3 0.0 copy-start.6
  62.3 22.2 %all_to_all.67 = bf16[64,8,128]{2,1,0:T(8,128)(2,1)S(1)} all-to-all(bf16[64,8,128]{2,1,0:T(8,128)(2,1)S(1)} %bitcast.28), channel_id=1, replica_groups=mesh['grid'=64,'dp'=8] {'grid'}, dimensions={0} | all-to-all | bytes 262144 | tf_op jit(solution)/shard_map/all_to_all | solution.py:312
  84.5 0.0 copy-done.4
  84.5 0.0 copy-done.6
  84.5 1.1 shard_map.152
  85.5 20.9 %all_to_all.68 = bf16[64,8,128]{2,1,0:T(8,128)(2,1)S(1)} all-to-all(bf16[64,8,128]{2,1,0:T(8,128)(2,1)S(1)} %bitcast.32), channel_id=1, replica_groups=mesh['grid'=64,'dp'=8] {'grid'}, dimensions={0} | all-to-all | bytes 262144 | tf_op jit(solution)/shard_map/all_to_all | solution.py:312
  106.4 1.0 shard_map.153
  107.4 0.0 copy-start.5
  107.4 21.0 %all_to_all.69 = bf16[64,8,128]{2,1,0:T(8,128)(2,1)S(1)} all-to-all(bf16[64,8,128]{2,1,0:T(8,128)(2,1)S(1)} %bitcast.31), channel_id=1, replica_groups=mesh['grid'=64,'dp'=8] {'grid'}, dimensions={0} | all-to-all | bytes 262144 | tf_op jit(solution)/shard_map/all_to_all | solution.py:312
  128.4 3.3 %all-to-all-start.5 = ((bf16[8,16,128]{2,1,0:T(8,128)(2,1)}), bf16[8,16,128]{2,1,0:T(8,128)(2,1)S(1)}, u32[]{:S(2)}, u32[]{:S(2)}) async-start(bf16[8,16,128]{2,1,0:T(8,128)(2,1)} %bitcast.16), calls=%async_computation.5 | async-start | bytes 65536 | tf_op jit(solution)/shard_map/all_to_all | solution.py:312
  131.7 0.0 copy-done.5
  131.7 0.0 copy-start.7
  131.8 1.3 shard_map.154
  133.1 5.2 %all-to-all-done.5 = bf16[8,16,128]{2,1,0:T(8,128)(2,1)S(1)} async-done(((bf16[8,16,128]{2,1,0:T(8,128)(2,1)}), bf16[8,16,128]{2,1,0:T(8,128)(2,1)S(1)}, u32[]{:S(2)}, u32[]{:S(2)}) %all-to-all-start.5) | async-done | bytes 32800 | tf_op jit(solution)/shard_map/all_to_all | solution.py:312
  138.3 0.0 copy-done.7
  138.3 1.9 %shard_map.155 = (f32[8,1,2,4096]{3,2,1,0:T(2,128)}, f32[8,1,2,4096]{3,2,1,0:T(2,128)}, f32[8,1,2,4096]{3,2,1,0:T(2,128)}) custom-call(bf16[128,128]{1,0:T(8,128)(2,1)S(1)} %bitcast.33, bf16[512,128]{1,0:T(8,128)(2,1)S(1)} %copy-done.7, f32[16,4096]{1,0:T(8,128)S(1)} %get-tuple-element.34.weight_ref, f32[16,4096]{1,0:T(8,128)S(1)} %get-tuple-element.35.first_ref, ...), custom_call_target="tpu_custom_call" | custom-call | tf_op jit(solution)/shard_map/pallas_call | solution.py:301
Async XLA Ops:
  3.2 18.2 %copy-start.8 = (f32[8,1,2,4096]{3,2,1,0:T(2,128)S(1)}, f32[8,1,2,4096]{3,2,1,0:T(2,128)}, u32[]{:S(2)}) copy-start(f32[8,1,2,4096]{3,2,1,0:T(2,128)} %weight_hbm.1) | copy-start | bytes 786436
  3.2 35.4 %all-to-all-start = ((bf16[64,8,128]{2,1,0:T(8,128)(2,1)}), bf16[64,8,128]{2,1,0:T(8,128)(2,1)S(1)}, u32[]{:S(2)}, u32[]{:S(2)}) async-start(bf16[64,8,128]{2,1,0:T(8,128)(2,1)} %bitcast.1), calls=%async_computation | async-start | bytes 262144 | tf_op jit(solution)/shard_map/all_to_all | solution.py:312
  38.6 6.5 %copy-start.10 = (f32[64]{0:T(128)S(1)}, f32[64]{0:T(128)}, u32[]{:S(2)}) copy-start(f32[64]{0:T(128)} %param.15) | copy-start | bytes 772
  38.6 7.5 %copy-start = (bf16[1,8,64,512]{3,2,1,0:T(8,128)(2,1)S(1)}, bf16[1,8,64,512]{3,2,1,0:T(8,128)(2,1)}, u32[]{:S(2)}) copy-start(bf16[1,8,64,512]{3,2,1,0:T(8,128)(2,1)} %param.12) | copy-start | bytes 1572868
  38.6 23.1 %all-to-all-start.1 = ((bf16[8,512,128]{2,1,0:T(8,128)(2,1)}), bf16[8,512,128]{2,1,0:T(8,128)(2,1)S(1)}, u32[]{:S(2)}, u32[]{:S(2)}) async-start(bf16[8,512,128]{2,1,0:T(8,128)(2,1)} %bitcast.7), calls=%async_computation.1 | async-start | bytes 2097152 | tf_op jit(solution)/shard_map/all_to_all | solution.py:312
  45.1 0.7 copy-start.9
  46.1 1.9 %copy-start.1 = (bf16[256,512]{1,0:T(8,128)(2,1)S(1)}, bf16[256,512]{1,0:T(8,128)(2,1)}, u32[]{:S(2)}) copy-start(bf16[256,512]{1,0:T(8,128)(2,1)} %constant.14.clone.to_modes_ref) | copy-start | bytes 786436
  47.2 0.8 copy-start.3
  48.0 13.7 %copy-start.2 = (bf16[512,256]{1,0:T(8,128)(2,1)S(1)}, bf16[512,256]{1,0:T(8,128)(2,1)}, u32[]{:S(2)}) copy-start(bf16[512,256]{1,0:T(8,128)(2,1)} %constant.15.clone.to_rows_ref) | copy-start | bytes 786436
  61.7 22.8 %copy-start.4 = (bf16[512,512]{1,0:T(8,128)(2,1)S(1)}, bf16[512,512]{1,0:T(8,128)(2,1)}, u32[]{:S(2)}) copy-start(bf16[512,512]{1,0:T(8,128)(2,1)} %copy-done.3) | copy-start | bytes 1572868
  62.3 22.2 %copy-start.6 = (bf16[128,512]{1,0:T(8,128)(2,1)S(1)}, bf16[128,512]{1,0:T(8,128)(2,1)}, u32[]{:S(2)}) copy-start(bf16[128,512]{1,0:T(8,128)(2,1)} %constant.13.clone.inverse_ref) | copy-start | bytes 393220
  107.4 24.4 %copy-start.5 = (bf16[128,512]{1,0:T(8,128)(2,1)S(1)}, bf16[128,512]{1,0:T(8,128)(2,1)}, u32[]{:S(2)}) copy-start(bf16[128,512]{1,0:T(8,128)(2,1)} %constant.12.clone.table_hbm.forward_ref) | copy-start | bytes 393220
  128.4 9.9 %all-to-all-start.5 = ((bf16[8,16,128]{2,1,0:T(8,128)(2,1)}), bf16[8,16,128]{2,1,0:T(8,128)(2,1)S(1)}, u32[]{:S(2)}, u32[]{:S(2)}) async-start(bf16[8,16,128]{2,1,0:T(8,128)(2,1)} %bitcast.16), calls=%async_computation.5 | async-start | bytes 65536 | tf_op jit(solution)/shard_map/all_to_all | solution.py:312
  131.7 6.5 %copy-start.7 = (bf16[512,128]{1,0:T(8,128)(2,1)S(1)}, bf16[512,128]{1,0:T(8,128)(2,1)}, u32[]{:S(2)}) copy-start(bf16[512,128]{1,0:T(8,128)(2,1)} %constant.16.clone.pick_ref) | copy-start | bytes 393220

commit v4 on v3

--- a/solution.py
+++ b/solution.py
@@ -18,6 +18,9 @@
 HALF = 64
 BLOCKS = 8
 
+GRID_ORDER = [(52 + 27 * k) % 64 for k in range(64)]
+DP_ORDER = [(k + 5) % 8 for k in range(8)]
+
 beta_one = 0.9
 beta_two = 0.999
 learn_rate = 0.01
@@ -29,7 +32,7 @@
 
 
 def tables():
-    frequency = np.arange(MY)
+    frequency = np.array(GRID_ORDER)
     position = np.arange(NY)
     angles = ((position[:, None] * frequency[None, :]) % NY).astype(np.float32) * np.float32(
         2.0 * math.pi / NY
@@ -45,7 +48,10 @@
     turn = ((wavenumber[:, None] * rows[None, :]) % NX).astype(np.float32) * np.float32(
         2.0 * math.pi / NX
     )
-    col_cos, col_sin = np.cos(turn), np.sin(turn)
+    by_order = lambda t: (
+        t.reshape(BLOCKS, 8, NX // SLAB, SLAB)[DP_ORDER][:, :, GRID_ORDER].reshape(MX, NX)
+    )
+    col_cos, col_sin = by_order(np.cos(turn)), by_order(np.sin(turn))
 
     by_slab = lambda t: t.reshape(BLOCKS, 8, NX // SLAB, QUAD, 2)
     c, s = by_slab(col_cos), by_slab(col_sin)
@@ -309,7 +315,10 @@
 
 
 def exchange(array, axis):
-    return lax.all_to_all(array, axis, split_axis=0, concat_axis=0, tiled=True)
+    groups = [GRID_ORDER if axis == "grid" else DP_ORDER]
+    return lax.all_to_all(
+        array, axis, split_axis=0, concat_axis=0, axis_index_groups=groups, tiled=True
+    )
 
 
 def shards(

time: 141 us -> 130 us (0.922)
  waiting for transfers between devices: 33.8 us -> 15.8 us
  starting transfers between devices: 28.1 us -> 36 us
  blocking collectives: 64 us -> 62.4 us
    all_to_all x3, waiting for transfers between devices: 33.8 us -> 15.8 us  [exchange(): lax.all_to_all(array, axis, split_axis=0, concat_axis=0, axis_index_group...]
    all_to_all x3, starting transfers between devices: 28.1 us -> 36 us  [exchange(): lax.all_to_all(array, axis, split_axis=0, concat_axis=0, axis_index_group...]
    all_to_all x3, blocking collectives: 64 us -> 62.4 us  [exchange(): lax.all_to_all(array, axis, split_axis=0, concat_axis=0, axis_index_group...]
where the time goes in v4:
time: 130 us; the launch traced here: 129 us
  blocking collectives  62.4 us (48%)
  starting transfers between devices  36 us (28%)
  waiting for transfers between devices  15.8 us (12%)
  Pallas kernels  11 us (8%)
  local copies, waits for them, and re-layouts  2.29 us (2%)
    all_to_all x3, blocking collectives, exchange(): lax.all_to_all(array, axis, split_axis=0, concat_axis=0, axis_index_group...  62.4 us
    all_to_all x3, starting transfers between devices, exchange(): lax.all_to_all(array, axis, split_axis=0, concat_axis=0, axis_index_group...  36 us
    all_to_all x3, waiting for transfers between devices, exchange(): lax.all_to_all(array, axis, split_axis=0, concat_axis=0, axis_index_group...  15.8 us
    pallas_call x9, Pallas kernels, call(): pl.pallas_call(kernel, out_shape=[place(shape, dtype) for shape, dtype in...  11 us
  transfers between devices with their start and end apart: 3, of which 3 were waited for; matrix products, arithmetic and copies ran while one was open for 1% of the time, Pallas kernels for 3%

profile of v4, /device:TPU:1, one launch (start us, length us, event | category | flops | bytes accessed | tf_op | source)
XLA Modules:
  0.0 128.6 jit_solution(1745307325512608881)
XLA Ops:
  0.6 2.6 %shard_map.147 = bf16[512,128]{1,0:T(8,128)(2,1)} custom-call(bf16[512,512]{1,0:T(8,128)(2,1)} %bitcast.24, bf16[128,512]{1,0:T(8,128)(2,1)} %constant.12.clone.table_hbm.forward_ref), custom_call_target="tpu_custom_call" | custom-call | tf_op jit(solution)/shard_map/pallas_call | solution.py:307
  3.2 0.0 copy-start.8
  3.2 20.0 %all-to-all-start = ((bf16[64,8,128]{2,1,0:T(8,128)(2,1)}), bf16[64,8,128]{2,1,0:T(8,128)(2,1)S(1)}, u32[]{:S(2)}, u32[]{:S(2)}) async-start(bf16[64,8,128]{2,1,0:T(8,128)(2,1)} %bitcast.1), calls=%async_computation | async-start | bytes 262144 | tf_op jit(solution)/shard_map/all_to_all | solution.py:319
  23.2 0.0 copy-done.8
  23.3 0.1 convert_element_type.3
  23.4 0.2 reshape.41
  23.6 0.3 copy.20
  23.9 0.1 reshape.42.local_ref
  24.0 1.1 shard_map.150
  25.1 6.5 %all-to-all-done = bf16[64,8,128]{2,1,0:T(8,128)(2,1)S(1)} async-done(((bf16[64,8,128]{2,1,0:T(8,128)(2,1)}), bf16[64,8,128]{2,1,0:T(8,128)(2,1)S(1)}, u32[]{:S(2)}, u32[]{:S(2)}) %all-to-all-start) | async-done | bytes 131104 | tf_op jit(solution)/shard_map/all_to_all | solution.py:319
  31.6 0.0 copy-start.10
  31.6 0.0 copy-start
  31.6 8.9 %all-to-all-start.1 = ((bf16[8,512,128]{2,1,0:T(8,128)(2,1)}), bf16[8,512,128]{2,1,0:T(8,128)(2,1)S(1)}, u32[]{:S(2)}, u32[]{:S(2)}) async-start(bf16[8,512,128]{2,1,0:T(8,128)(2,1)} %bitcast.7), calls=%async_computation.1 | async-start | bytes 2097152 | tf_op jit(solution)/shard_map/all_to_all | solution.py:319
  40.6 0.0 copy-done.10
  40.6 0.1 maximum_bitcast_fusion
  40.6 0.0 copy-start.9
  40.6 0.1 copy.17.bias_ref
  40.8 0.6 copy-done.9
  41.4 0.1 fusion.2
  41.4 0.1 copy.16.point_ref
  41.6 0.0 copy-done
  41.6 0.0 copy-start.1
  41.6 1.1 shard_map.149
  42.7 0.0 copy-start.3
  42.7 0.8 copy-done.3
  43.5 0.0 copy-start.2
  43.5 0.0 copy-done.1
  43.5 0.3 shard_map.148.modes_ref
  43.8 8.9 %all-to-all-done.1 = bf16[8,512,128]{2,1,0:T(8,128)(2,1)S(1)} async-done(((bf16[8,512,128]{2,1,0:T(8,128)(2,1)}), bf16[8,512,128]{2,1,0:T(8,128)(2,1)S(1)}, u32[]{:S(2)}, u32[]{:S(2)}) %all-to-all-start.1) | async-done | bytes 1048608 | tf_op jit(solution)/shard_map/all_to_all | solution.py:319
  52.7 0.0 copy-done.2
  52.7 0.0 copy-start.4
  52.7 0.6 shard_map.151
  53.3 0.0 copy-start.6
  53.3 21.5 %all_to_all.67 = bf16[64,8,128]{2,1,0:T(8,128)(2,1)S(1)} all-to-all(bf16[64,8,128]{2,1,0:T(8,128)(2,1)S(1)} %bitcast.28), channel_id=1, replica_groups={{416,120,336,40,256,472,176,392,96,312,16,232,448,152,368,72,288,504,20..., dimensions={0} | all-to-all | bytes 262144 | tf_op jit(solution)/shard_map/all_to_all | solution.py:319
  74.8 0.0 copy-done.4
  74.8 0.0 copy-done.6
  74.8 1.1 shard_map.152
  75.9 20.4 %all_to_all.68 = bf16[64,8,128]{2,1,0:T(8,128)(2,1)S(1)} all-to-all(bf16[64,8,128]{2,1,0:T(8,128)(2,1)S(1)} %bitcast.32), channel_id=1, replica_groups={{416,120,336,40,256,472,176,392,96,312,16,232,448,152,368,72,288,504,20..., dimensions={0} | all-to-all | bytes 262144 | tf_op jit(solution)/shard_map/all_to_all | solution.py:319
  96.3 1.0 shard_map.153
  97.3 0.0 copy-start.5
  97.3 20.5 %all_to_all.69 = bf16[64,8,128]{2,1,0:T(8,128)(2,1)S(1)} all-to-all(bf16[64,8,128]{2,1,0:T(8,128)(2,1)S(1)} %bitcast.31), channel_id=1, replica_groups={{416,120,336,40,256,472,176,392,96,312,16,232,448,152,368,72,288,504,20..., dimensions={0} | all-to-all | bytes 262144 | tf_op jit(solution)/shard_map/all_to_all | solution.py:319
  117.8 7.1 %all-to-all-start.5 = ((bf16[8,16,128]{2,1,0:T(8,128)(2,1)}), bf16[8,16,128]{2,1,0:T(8,128)(2,1)S(1)}, u32[]{:S(2)}, u32[]{:S(2)}) async-start(bf16[8,16,128]{2,1,0:T(8,128)(2,1)} %bitcast.16), calls=%async_computation.5 | async-start | bytes 65536 | tf_op jit(solution)/shard_map/all_to_all | solution.py:319
  124.9 0.0 copy-done.5
  124.9 0.0 copy-start.7
  124.9 1.3 %shard_map.154 = (bf16[512,512]{1,0:T(8,128)(2,1)}, f32[16,4096]{1,0:T(8,128)S(1)}, f32[16,4096]{1,0:T(8,128)S(1)}, f32[16,4096]{1,0:T(8,128)S(1)}) custom-call(bf16[512,128]{1,0:T(8,128)(2,1)S(1)} %bitcast.27, bf16[512,512]{1,0:T(8,128)(2,1)S(1)} %get-tuple-element.31.grad_ref, bf16[128,128]{1,0:T(8,128)(2,1)S(1)} %get-tuple-element.40.point_ref, ...), custom_call_target="tpu_custom_call" | custom-call | tf_op jit(solution)/shard_map/pallas_call | solution.py:307
  126.2 0.5 all-to-all-done.5
  126.7 0.0 copy-done.7
  126.7 1.9 %shard_map.155 = (f32[8,1,2,4096]{3,2,1,0:T(2,128)}, f32[8,1,2,4096]{3,2,1,0:T(2,128)}, f32[8,1,2,4096]{3,2,1,0:T(2,128)}) custom-call(bf16[128,128]{1,0:T(8,128)(2,1)S(1)} %bitcast.33, bf16[512,128]{1,0:T(8,128)(2,1)S(1)} %copy-done.7, f32[16,4096]{1,0:T(8,128)S(1)} %get-tuple-element.34.weight_ref, f32[16,4096]{1,0:T(8,128)S(1)} %get-tuple-element.35.first_ref, ...), custom_call_target="tpu_custom_call" | custom-call | tf_op jit(solution)/shard_map/pallas_call | solution.py:307
Async XLA Ops:
  3.2 20.1 %copy-start.8 = (f32[8,1,2,4096]{3,2,1,0:T(2,128)S(1)}, f32[8,1,2,4096]{3,2,1,0:T(2,128)}, u32[]{:S(2)}) copy-start(f32[8,1,2,4096]{3,2,1,0:T(2,128)} %weight_hbm.1) | copy-start | bytes 786436
  3.2 28.4 %all-to-all-start = ((bf16[64,8,128]{2,1,0:T(8,128)(2,1)}), bf16[64,8,128]{2,1,0:T(8,128)(2,1)S(1)}, u32[]{:S(2)}, u32[]{:S(2)}) async-start(bf16[64,8,128]{2,1,0:T(8,128)(2,1)} %bitcast.1), calls=%async_computation | async-start | bytes 262144 | tf_op jit(solution)/shard_map/all_to_all | solution.py:319
  31.6 9.0 %copy-start.10 = (f32[64]{0:T(128)S(1)}, f32[64]{0:T(128)}, u32[]{:S(2)}) copy-start(f32[64]{0:T(128)} %param.15) | copy-start | bytes 772
  31.6 9.9 %copy-start = (bf16[1,8,64,512]{3,2,1,0:T(8,128)(2,1)S(1)}, bf16[1,8,64,512]{3,2,1,0:T(8,128)(2,1)}, u32[]{:S(2)}) copy-start(bf16[1,8,64,512]{3,2,1,0:T(8,128)(2,1)} %param.12) | copy-start | bytes 1572868
  31.6 21.1 %all-to-all-start.1 = ((bf16[8,512,128]{2,1,0:T(8,128)(2,1)}), bf16[8,512,128]{2,1,0:T(8,128)(2,1)S(1)}, u32[]{:S(2)}, u32[]{:S(2)}) async-start(bf16[8,512,128]{2,1,0:T(8,128)(2,1)} %bitcast.7), calls=%async_computation.1 | async-start | bytes 2097152 | tf_op jit(solution)/shard_map/all_to_all | solution.py:319
  40.6 0.7 copy-start.9
  41.6 1.9 %copy-start.1 = (bf16[256,512]{1,0:T(8,128)(2,1)S(1)}, bf16[256,512]{1,0:T(8,128)(2,1)}, u32[]{:S(2)}) copy-start(bf16[256,512]{1,0:T(8,128)(2,1)} %constant.14.clone.to_modes_ref) | copy-start | bytes 786436
  42.7 0.8 copy-start.3
  43.5 9.2 %copy-start.2 = (bf16[512,256]{1,0:T(8,128)(2,1)S(1)}, bf16[512,256]{1,0:T(8,128)(2,1)}, u32[]{:S(2)}) copy-start(bf16[512,256]{1,0:T(8,128)(2,1)} %constant.15.clone.to_rows_ref) | copy-start | bytes 786436
  52.7 22.1 %copy-start.4 = (bf16[512,512]{1,0:T(8,128)(2,1)S(1)}, bf16[512,512]{1,0:T(8,128)(2,1)}, u32[]{:S(2)}) copy-start(bf16[512,512]{1,0:T(8,128)(2,1)} %copy-done.3) | copy-start | bytes 1572868
  53.3 21.5 %copy-start.6 = (bf16[128,512]{1,0:T(8,128)(2,1)S(1)}, bf16[128,512]{1,0:T(8,128)(2,1)}, u32[]{:S(2)}) copy-start(bf16[128,512]{1,0:T(8,128)(2,1)} %constant.13.clone.inverse_ref) | copy-start | bytes 393220
  97.3 27.6 %copy-start.5 = (bf16[128,512]{1,0:T(8,128)(2,1)S(1)}, bf16[128,512]{1,0:T(8,128)(2,1)}, u32[]{:S(2)}) copy-start(bf16[128,512]{1,0:T(8,128)(2,1)} %constant.12.clone.table_hbm.forward_ref) | copy-start | bytes 393220
  117.8 8.9 %all-to-all-start.5 = ((bf16[8,16,128]{2,1,0:T(8,128)(2,1)}), bf16[8,16,128]{2,1,0:T(8,128)(2,1)S(1)}, u32[]{:S(2)}, u32[]{:S(2)}) async-start(bf16[8,16,128]{2,1,0:T(8,128)(2,1)} %bitcast.16), calls=%async_computation.5 | async-start | bytes 65536 | tf_op jit(solution)/shard_map/all_to_all | solution.py:319
  124.9 1.8 %copy-start.7 = (bf16[512,128]{1,0:T(8,128)(2,1)S(1)}, bf16[512,128]{1,0:T(8,128)(2,1)}, u32[]{:S(2)}) copy-start(bf16[512,128]{1,0:T(8,128)(2,1)} %constant.16.clone.pick_ref) | copy-start | bytes 393220

commit v5 on v4

--- a/solution.py
+++ b/solution.py
@@ -63,15 +63,11 @@
     to_rows = np.stack([np.stack([c, -s], 0), np.stack([s, c], 0)], 0)
     to_rows = to_rows.transpose(3, 0, 4, 1, 5, 2).reshape(512, 256)
 
-    pick = np.zeros((4, 8, 8, 2, 8, 2, 8), np.float32)
-    for b in range(8):
-        for j in range(8):
-            for p in range(2):
-                pick[0, b, j, p, b, 0, j] = 1.0
-                pick[1, b, j, p, b, 1, j] = 1.0
-                pick[2, b, j, p, b, p, j] = 1.0
-                pick[3, b, j, p, b, 1 - p, j] = 1.0 - 2.0 * p
-    pick = pick.reshape(512, 128)
+    pick = np.zeros((2, 128, 2, C // 2, 2), np.float32)
+    for c in range(C):
+        for p in range(2):
+            pick[p, c, c % 2, c // 2, p] = 1.0
+    pick = pick.reshape(256, 128)
     made = (forward, inverse, to_modes, to_rows, pick)
     return tuple(np.asarray(t, np.float32).astype(jnp.bfloat16) for t in made)
 
@@ -238,12 +234,13 @@
     second_out,
     out_ref,
     woven_ref,
-    masters_ref,
     sems,
 ):
     loads = []
-    for n, source in enumerate((weight_hbm, first_hbm, second_hbm)):
-        copy = pltpu.make_async_copy(source, masters_ref.at[n], sems.at[QUAD + n])
+    for n, (source, target) in enumerate(
+        ((weight_hbm, weight_out), (first_hbm, first_out), (second_hbm, second_out))
+    ):
+        copy = pltpu.make_async_copy(source, target, sems.at[QUAD + n])
         copy.start()
         loads.append(copy)
     forward = forward_ref[...]
@@ -256,42 +253,57 @@
         copy = pltpu.make_async_copy(out_ref.at[part(q)], out_hbm.at[part(q)], sems.at[q])
         copy.start()
         copies.append(copy)
-    for n, target in enumerate((weight_out, first_out, second_out)):
-        loads[n].wait()
-        for j in range(8):
-            target[2 * j : 2 * j + 2, :] = masters_ref[n, j, 0]
+    for copy in loads + copies:
+        copy.wait()
+
+
+def adam_kernel(
+    pair_ref,
+    pick_ref,
+    weight_ref,
+    first_ref,
+    second_ref,
+    new_weight_hbm,
+    new_first_hbm,
+    new_second_hbm,
+    made_ref,
+    sems,
+):
+    bias_one = 1.0 - beta_one**adam_step
+    bias_two = 1.0 - beta_two**adam_step
+    wide = pair_ref[...].astype(f32)
+    turned = []
+    for sample in range(8):
+        turned.append(-wide[sample * 16 + 8 : sample * 16 + 16])
+        turned.append(wide[sample * 16 : sample * 16 + 8])
+    both = jnp.concatenate([wide, jnp.concatenate(turned, axis=0)], axis=1).astype(bf16)
+    left = mm(both, pick_ref[...])
+    left = jnp.concatenate([left, swap(left)], axis=0).astype(bf16)
+    low = low_lanes((128, 128))
+    right = jnp.concatenate([jnp.where(low, swap(wide), 0.0), jnp.where(low, 0.0, wide)], axis=0)
+    mode = lax.broadcasted_iota(jnp.int32, (256, 128), 0) % 8
+    spread = [jnp.where(mode == j, right, 0.0).astype(bf16) for j in range(8)]
+    gradients = mm_tn(left, jnp.concatenate(spread, axis=1))
+    copies = []
+    for j in range(8):
+        at = slice(j * 64, (j + 1) * 64)
+        gradient = gradients[:64, j * 128 : (j + 1) * 128]
+        first = beta_one * first_ref[at, :] + (1.0 - beta_one) * gradient
+        second = beta_two * second_ref[at, :] + (1.0 - beta_two) * gradient * gradient
+        step = learn_rate * (first / bias_one) / (jnp.sqrt(second / bias_two) + epsilon_adam)
+        made_ref[0, at, :] = weight_ref[at, :] - step
+        made_ref[1, at, :] = first
+        made_ref[2, at, :] = second
+        if j % 2 == 1:
+            at = slice((j - 1) * 64, (j + 1) * 64)
+            for n, target in enumerate((new_weight_hbm, new_first_hbm, new_second_hbm)):
+                copy = pltpu.make_async_copy(
+                    made_ref.at[n, at], target.at[at], sems.at[3 * (j // 2) + n]
+                )
+                copy.start()
+                copies.append(copy)
     for copy in copies:
         copy.wait()
-
-
-def adam_kernel(
-    pair_ref, pick_ref, weight_ref, first_ref, second_ref, new_weight_ref, new_first_ref, new_second_ref
-):
-    width = 512
-    bias_one = 1.0 - beta_one**adam_step
-    bias_two = 1.0 - beta_two**adam_step
-    picked = mm(pick_ref[...], pair_ref[...]).astype(bf16)
-    row = lax.broadcasted_iota(jnp.int32, (128, width), 0)
-    lane = lax.broadcasted_iota(jnp.int32, (128, width), 1)
-    outer = jnp.where(row == HALF + lane % HALF, 1.0, 0.0).astype(bf16)
-    right_one = mm(picked[256:384], outer)
-    right_two = mm(picked[384:], outer)
-    for n in range(C * C // width):
-        inner = jnp.where(row == n * (width // HALF) + lane // HALF, 1.0, 0.0).astype(bf16)
-        product = mm(picked[:128], inner) * right_one + mm(picked[128:256], inner) * right_two
-        gradient = product[:16]
-        for b in range(1, 8):
-            gradient = gradient + product[b * 16 : (b + 1) * 16]
-        at = slice(n * width, (n + 1) * width)
-        first = beta_one * first_ref[:, at] + (1.0 - beta_one) * gradient
-        second = beta_two * second_ref[:, at] + (1.0 - beta_two) * gradient * gradient
-        step = learn_rate * (first / bias_one) / (jnp.sqrt(second / bias_two) + epsilon_adam)
-        weight = weight_ref[:, at] - step
-        for j in range(8):
-            rows = slice(2 * j, 2 * j + 2)
-            new_weight_ref[j, 0, :, at] = weight[rows]
-            new_first_ref[j, 0, :, at] = first[rows]
-            new_second_ref[j, 0, :, at] = second[rows]
 
 
 HBM = pl.BlockSpec(memory_space=pltpu.HBM)
@@ -386,11 +398,14 @@
     )
     received, pair = lax.optimization_barrier((exchange(sent, "grid"), pair))
     pair = exchange(pair, "dp")
-    masters = (spectral_weight, first_moment, second_moment)
-    shape = spectral_weight.shape
-    grad_field, *flat = call(
+    masters = [
+        m.reshape(8, 2, C // 2, 128).transpose(0, 2, 1, 3).reshape(512, 128)
+        for m in (spectral_weight, first_moment, second_moment)
+    ]
+    flat = [((512, 128), f32)] * 3
+    grad_field, *near = call(
         field_kernel,
-        [((512, 512), bf16)] + [((16, C * C), f32)] * 3,
+        [((512, 512), bf16)] + flat,
         received,
         pre_grad,
         point,
@@ -398,9 +413,21 @@
         *masters,
         far=(4, 5, 6),
         far_out=(0,),
-        scratch=(plane, woven, pltpu.VMEM((3,) + shape, f32), dma((QUAD + 3,))),
-    )
-    new_weight, new_first, new_second = call(adam_kernel, [(shape, f32)] * 3, pair, pick, *flat)
+        scratch=(plane, woven, dma((QUAD + 3,))),
+    )
+    made = call(
+        adam_kernel,
+        flat,
+        pair,
+        pick,
+        *near,
+        far_out=(0, 1, 2),
+        scratch=(pltpu.VMEM((3, 512, 128), f32), dma((12,))),
+    )
+    new_weight, new_first, new_second = (
+        m.reshape(8, C // 2, 2, 128).transpose(0, 2, 1, 3).reshape(spectral_weight.shape)
+        for m in made
+    )
     return (grad_field.reshape(in_field.shape), new_weight, new_first, new_second)
 
 

time: 130 us -> 129 us (level)
  no operation moved by 1% of the time
where the time goes in v5:
time: 129 us; the launch traced here: 128 us
  blocking collectives  62.4 us (48%)
  starting transfers between devices  36 us (28%)
  waiting for transfers between devices  15.9 us (12%)
  Pallas kernels  10.4 us (8%)
  local copies, waits for them, and re-layouts  2.29 us (2%)
    all_to_all x3, blocking collectives, exchange(): lax.all_to_all(array, axis, split_axis=0, concat_axis=0, axis_index_group...  62.4 us
    all_to_all x3, starting transfers between devices, exchange(): lax.all_to_all(array, axis, split_axis=0, concat_axis=0, axis_index_group...  36 us
    all_to_all x3, waiting for transfers between devices, exchange(): lax.all_to_all(array, axis, split_axis=0, concat_axis=0, axis_index_group...  15.9 us
    pallas_call x9, Pallas kernels, call(): pl.pallas_call(kernel, out_shape=[place(shape, dtype) for shape, dtype in...  10.4 us
  transfers between devices with their start and end apart: 3, of which 3 were waited for; matrix products, arithmetic and copies ran while one was open for 1% of the time, Pallas kernels for 3%

profile of v5, /device:TPU:1, one launch (start us, length us, event | category | flops | bytes accessed | tf_op | source)
XLA Modules:
  0.0 128.2 jit_solution(13072970282513743788)
XLA Ops:
  0.6 2.6 %shard_map.147 = bf16[512,128]{1,0:T(8,128)(2,1)} custom-call(bf16[512,512]{1,0:T(8,128)(2,1)} %bitcast.54, bf16[128,512]{1,0:T(8,128)(2,1)} %constant.12.clone.table_hbm.forward_ref), custom_call_target="tpu_custom_call" | custom-call | tf_op jit(solution)/shard_map/pallas_call | solution.py:319
  3.2 0.0 copy-start.8
  3.2 20.0 %all-to-all-start = ((bf16[64,8,128]{2,1,0:T(8,128)(2,1)}), bf16[64,8,128]{2,1,0:T(8,128)(2,1)S(1)}, u32[]{:S(2)}, u32[]{:S(2)}) async-start(bf16[64,8,128]{2,1,0:T(8,128)(2,1)} %bitcast.1), calls=%async_computation | async-start | bytes 262144 | tf_op jit(solution)/shard_map/all_to_all | solution.py:331
  23.2 0.0 copy-done.8
  23.3 0.1 convert_element_type.3
  23.4 0.2 reshape.77
  23.6 0.3 copy.26
  23.9 0.1 reshape.78.local_ref
  24.0 1.1 shard_map.150
  25.1 6.5 %all-to-all-done = bf16[64,8,128]{2,1,0:T(8,128)(2,1)S(1)} async-done(((bf16[64,8,128]{2,1,0:T(8,128)(2,1)}), bf16[64,8,128]{2,1,0:T(8,128)(2,1)S(1)}, u32[]{:S(2)}, u32[]{:S(2)}) %all-to-all-start) | async-done | bytes 131104 | tf_op jit(solution)/shard_map/all_to_all | solution.py:331
  31.6 0.0 copy-start.10
  31.6 0.0 copy-start
  31.6 8.9 %all-to-all-start.1 = ((bf16[8,512,128]{2,1,0:T(8,128)(2,1)}), bf16[8,512,128]{2,1,0:T(8,128)(2,1)S(1)}, u32[]{:S(2)}, u32[]{:S(2)}) async-start(bf16[8,512,128]{2,1,0:T(8,128)(2,1)} %bitcast.7), calls=%async_computation.1 | async-start | bytes 2097152 | tf_op jit(solution)/shard_map/all_to_all | solution.py:331
  40.6 0.0 copy-done.10
  40.6 0.1 maximum_bitcast_fusion
  40.6 0.0 copy-start.9
  40.6 0.1 copy.17.bias_ref
  40.8 0.6 copy-done.9
  41.4 0.1 fusion.2
  41.4 0.1 copy.16.point_ref
  41.6 0.0 copy-done
  41.6 0.0 copy-start.1
  41.6 1.1 shard_map.149
  42.7 0.0 copy-start.3
  42.7 0.8 copy-done.3
  43.5 0.0 copy-start.2
  43.5 0.0 copy-done.1
  43.5 0.3 shard_map.148.modes_ref
  43.8 8.9 %all-to-all-done.1 = bf16[8,512,128]{2,1,0:T(8,128)(2,1)S(1)} async-done(((bf16[8,512,128]{2,1,0:T(8,128)(2,1)}), bf16[8,512,128]{2,1,0:T(8,128)(2,1)S(1)}, u32[]{:S(2)}, u32[]{:S(2)}) %all-to-all-start.1) | async-done | bytes 1048608 | tf_op jit(solution)/shard_map/all_to_all | solution.py:331
  52.7 0.0 copy-done.2
  52.7 0.0 copy-start.4
  52.7 0.6 shard_map.151
  53.3 0.0 copy-start.6
  53.3 21.5 %all_to_all.67 = bf16[64,8,128]{2,1,0:T(8,128)(2,1)S(1)} all-to-all(bf16[64,8,128]{2,1,0:T(8,128)(2,1)S(1)} %bitcast.58), channel_id=1, replica_groups={{416,120,336,40,256,472,176,392,96,312,16,232,448,152,368,72,288,504,20..., dimensions={0} | all-to-all | bytes 262144 | tf_op jit(solution)/shard_map/all_to_all | solution.py:331
  74.8 0.0 copy-done.4
  74.8 0.0 copy-done.6
  74.8 1.1 shard_map.152
  75.9 20.4 %all_to_all.68 = bf16[64,8,128]{2,1,0:T(8,128)(2,1)S(1)} all-to-all(bf16[64,8,128]{2,1,0:T(8,128)(2,1)S(1)} %bitcast.63), channel_id=1, replica_groups={{416,120,336,40,256,472,176,392,96,312,16,232,448,152,368,72,288,504,20..., dimensions={0} | all-to-all | bytes 262144 | tf_op jit(solution)/shard_map/all_to_all | solution.py:331
  96.3 1.0 shard_map.153
  97.3 0.0 copy-start.5
  97.3 20.5 %all_to_all.69 = bf16[64,8,128]{2,1,0:T(8,128)(2,1)S(1)} all-to-all(bf16[64,8,128]{2,1,0:T(8,128)(2,1)S(1)} %bitcast.62), channel_id=1, replica_groups={{416,120,336,40,256,472,176,392,96,312,16,232,448,152,368,72,288,504,20..., dimensions={0} | all-to-all | bytes 262144 | tf_op jit(solution)/shard_map/all_to_all | solution.py:331
  117.8 7.1 %all-to-all-start.5 = ((bf16[8,16,128]{2,1,0:T(8,128)(2,1)}), bf16[8,16,128]{2,1,0:T(8,128)(2,1)S(1)}, u32[]{:S(2)}, u32[]{:S(2)}) async-start(bf16[8,16,128]{2,1,0:T(8,128)(2,1)} %bitcast.25), calls=%async_computation.5 | async-start | bytes 65536 | tf_op jit(solution)/shard_map/all_to_all | solution.py:331
  124.9 0.0 copy-done.5
  124.9 0.0 copy-start.7
  124.9 1.3 shard_map.154
  126.1 0.6 all-to-all-done.5
  126.7 0.0 copy-done.7
  126.7 1.5 %shard_map.155 = (f32[512,128]{1,0:T(8,128)}, f32[512,128]{1,0:T(8,128)}, f32[512,128]{1,0:T(8,128)}) custom-call(bf16[128,128]{1,0:T(8,128)(2,1)S(1)} %bitcast.61, bf16[256,128]{1,0:T(8,128)(2,1)S(1)} %copy-done.7, f32[512,128]{1,0:T(8,128)S(1)} %get-tuple-element.34.weight_ref, f32[512,128]{1,0:T(8,128)S(1)} %get-tuple-element.35.first_ref, ...), custom_call_target="tpu_custom_call" | custom-call | tf_op jit(solution)/shard_map/pallas_call | solution.py:319
Async XLA Ops:
  3.2 20.1 %copy-start.8 = (f32[8,1,2,4096]{3,2,1,0:T(2,128)S(1)}, f32[8,1,2,4096]{3,2,1,0:T(2,128)}, u32[]{:S(2)}) copy-start(f32[8,1,2,4096]{3,2,1,0:T(2,128)} %param.16) | copy-start | bytes 786436
  3.2 28.4 %all-to-all-start = ((bf16[64,8,128]{2,1,0:T(8,128)(2,1)}), bf16[64,8,128]{2,1,0:T(8,128)(2,1)S(1)}, u32[]{:S(2)}, u32[]{:S(2)}) async-start(bf16[64,8,128]{2,1,0:T(8,128)(2,1)} %bitcast.1), calls=%async_computation | async-start | bytes 262144 | tf_op jit(solution)/shard_map/all_to_all | solution.py:331
  31.6 9.0 %copy-start.10 = (f32[64]{0:T(128)S(1)}, f32[64]{0:T(128)}, u32[]{:S(2)}) copy-start(f32[64]{0:T(128)} %param.15) | copy-start | bytes 772
  31.6 9.9 %copy-start = (bf16[1,8,64,512]{3,2,1,0:T(8,128)(2,1)S(1)}, bf16[1,8,64,512]{3,2,1,0:T(8,128)(2,1)}, u32[]{:S(2)}) copy-start(bf16[1,8,64,512]{3,2,1,0:T(8,128)(2,1)} %param.12) | copy-start | bytes 1572868
  31.6 21.1 %all-to-all-start.1 = ((bf16[8,512,128]{2,1,0:T(8,128)(2,1)}), bf16[8,512,128]{2,1,0:T(8,128)(2,1)S(1)}, u32[]{:S(2)}, u32[]{:S(2)}) async-start(bf16[8,512,128]{2,1,0:T(8,128)(2,1)} %bitcast.7), calls=%async_computation.1 | async-start | bytes 2097152 | tf_op jit(solution)/shard_map/all_to_all | solution.py:331
  40.6 0.7 copy-start.9
  41.6 1.9 %copy-start.1 = (bf16[256,512]{1,0:T(8,128)(2,1)S(1)}, bf16[256,512]{1,0:T(8,128)(2,1)}, u32[]{:S(2)}) copy-start(bf16[256,512]{1,0:T(8,128)(2,1)} %constant.14.clone.to_modes_ref) | copy-start | bytes 786436
  42.7 0.8 copy-start.3
  43.5 9.2 %copy-start.2 = (bf16[512,256]{1,0:T(8,128)(2,1)S(1)}, bf16[512,256]{1,0:T(8,128)(2,1)}, u32[]{:S(2)}) copy-start(bf16[512,256]{1,0:T(8,128)(2,1)} %constant.15.clone.to_rows_ref) | copy-start | bytes 786436
  52.7 22.1 %copy-start.4 = (bf16[512,512]{1,0:T(8,128)(2,1)S(1)}, bf16[512,512]{1,0:T(8,128)(2,1)}, u32[]{:S(2)}) copy-start(bf16[512,512]{1,0:T(8,128)(2,1)} %copy-done.3) | copy-start | bytes 1572868
  53.3 21.5 %copy-start.6 = (bf16[128,512]{1,0:T(8,128)(2,1)S(1)}, bf16[128,512]{1,0:T(8,128)(2,1)}, u32[]{:S(2)}) copy-start(bf16[128,512]{1,0:T(8,128)(2,1)} %constant.13.clone.inverse_ref) | copy-start | bytes 393220
  97.3 27.6 %copy-start.5 = (bf16[128,512]{1,0:T(8,128)(2,1)S(1)}, bf16[128,512]{1,0:T(8,128)(2,1)}, u32[]{:S(2)}) copy-start(bf16[128,512]{1,0:T(8,128)(2,1)} %constant.12.clone.table_hbm.forward_ref) | copy-start | bytes 393220
  117.8 8.9 %all-to-all-start.5 = ((bf16[8,16,128]{2,1,0:T(8,128)(2,1)}), bf16[8,16,128]{2,1,0:T(8,128)(2,1)S(1)}, u32[]{:S(2)}, u32[]{:S(2)}) async-start(bf16[8,16,128]{2,1,0:T(8,128)(2,1)} %bitcast.25), calls=%async_computation.5 | async-start | bytes 65536 | tf_op jit(solution)/shard_map/all_to_all | solution.py:331
  124.9 1.8 %copy-start.7 = (bf16[256,128]{1,0:T(8,128)(2,1)S(1)}, bf16[256,128]{1,0:T(8,128)(2,1)}, u32[]{:S(2)}) copy-start(bf16[256,128]{1,0:T(8,128)(2,1)} %constant.16.clone.pick_ref) | copy-start | bytes 196612

commit v6 on v5

--- a/solution.py
+++ b/solution.py
@@ -18,8 +18,8 @@
 HALF = 64
 BLOCKS = 8
 
-GRID_ORDER = [(52 + 27 * k) % 64 for k in range(64)]
-DP_ORDER = [(k + 5) % 8 for k in range(8)]
+GRID_ORDER = [(52 + 45 * k) % 64 for k in range(64)]
+DP_ORDER = [(5 + 3 * k) % 8 for k in range(8)]
 
 beta_one = 0.9
 beta_two = 0.999
@@ -135,18 +135,16 @@
 
 
 def spectra_kernel(field_hbm, table_hbm, out_ref, field_ref, table_ref, woven_ref, sems):
-    table_copy = pltpu.make_async_copy(table_hbm, table_ref, sems.at[QUAD])
-    table_copy.start()
     copies = [
-        pltpu.make_async_copy(field_hbm.at[part(q)], field_ref.at[part(q)], sems.at[q])
-        for q in range(QUAD)
+        pltpu.make_async_copy(field_hbm, field_ref, sems.at[0]),
+        pltpu.make_async_copy(table_hbm, table_ref, sems.at[1]),
     ]
     for copy in copies:
         copy.start()
-    table_copy.wait()
+    for copy in copies:
+        copy.wait()
     table = table_ref[...]
     for q in range(QUAD):
-        copies[q].wait()
         woven_ref[quarter(q), :] = mm_nt(table, field_ref[part(q), :])
     out_ref[...] = woven_ref[...].astype(bf16)
 
@@ -354,7 +352,7 @@
         field,
         forward,
         far=(0, 1),
-        scratch=(plane, pltpu.VMEM((128, 512), bf16), woven, dma((QUAD + 1,))),
+        scratch=(plane, pltpu.VMEM((128, 512), bf16), woven, dma((2,))),
     )
     columns = exchange(sent, "grid")
 

time: 129 us -> 129 us (level)
  no operation moved by 1% of the time
where the time goes in v6:
time: 129 us; the launch traced here: 128 us
  blocking collectives  62.3 us (48%)
  starting transfers between devices  36 us (28%)
  waiting for transfers between devices  16.1 us (12%)
  Pallas kernels  9.94 us (8%)
  local copies, waits for them, and re-layouts  2.29 us (2%)
    all_to_all x3, blocking collectives, exchange(): lax.all_to_all(array, axis, split_axis=0, concat_axis=0, axis_index_group...  62.3 us
    all_to_all x3, starting transfers between devices, exchange(): lax.all_to_all(array, axis, split_axis=0, concat_axis=0, axis_index_group...  36 us
    all_to_all x3, waiting for transfers between devices, exchange(): lax.all_to_all(array, axis, split_axis=0, concat_axis=0, axis_index_group...  16.1 us
    pallas_call x9, Pallas kernels, call(): pl.pallas_call(kernel, out_shape=[place(shape, dtype) for shape, dtype in...  9.94 us
  transfers between devices with their start and end apart: 3, of which 3 were waited for; matrix products, arithmetic and copies ran while one was open for 1% of the time, Pallas kernels for 3%

profile of v6, /device:TPU:1, one launch (start us, length us, event | category | flops | bytes accessed | tf_op | source)
XLA Modules:
  0.0 127.6 jit_solution(13495831341665489093)
XLA Ops:
  0.6 2.1 %shard_map.147 = bf16[512,128]{1,0:T(8,128)(2,1)} custom-call(bf16[512,512]{1,0:T(8,128)(2,1)} %bitcast.54, bf16[128,512]{1,0:T(8,128)(2,1)} %constant.12.clone.table_hbm.forward_ref), custom_call_target="tpu_custom_call" | custom-call | tf_op jit(solution)/shard_map/pallas_call | solution.py:317
  2.7 0.0 copy-start.8
  2.7 19.9 %all-to-all-start = ((bf16[64,8,128]{2,1,0:T(8,128)(2,1)}), bf16[64,8,128]{2,1,0:T(8,128)(2,1)S(1)}, u32[]{:S(2)}, u32[]{:S(2)}) async-start(bf16[64,8,128]{2,1,0:T(8,128)(2,1)} %bitcast.1), calls=%async_computation | async-start | bytes 262144 | tf_op jit(solution)/shard_map/all_to_all | solution.py:329
  22.6 0.0 copy-done.8
  22.6 0.1 convert_element_type.3
  22.7 0.2 reshape.77
  22.9 0.3 copy.26
  23.2 0.1 reshape.78.local_ref
  23.4 1.1 shard_map.150
  24.5 6.6 %all-to-all-done = bf16[64,8,128]{2,1,0:T(8,128)(2,1)S(1)} async-done(((bf16[64,8,128]{2,1,0:T(8,128)(2,1)}), bf16[64,8,128]{2,1,0:T(8,128)(2,1)S(1)}, u32[]{:S(2)}, u32[]{:S(2)}) %all-to-all-start) | async-done | bytes 131104 | tf_op jit(solution)/shard_map/all_to_all | solution.py:329
  31.1 0.0 copy-start.10
  31.1 0.0 copy-start
  31.1 8.9 %all-to-all-start.1 = ((bf16[8,512,128]{2,1,0:T(8,128)(2,1)}), bf16[8,512,128]{2,1,0:T(8,128)(2,1)S(1)}, u32[]{:S(2)}, u32[]{:S(2)}) async-start(bf16[8,512,128]{2,1,0:T(8,128)(2,1)} %bitcast.7), calls=%async_computation.1 | async-start | bytes 2097152 | tf_op jit(solution)/shard_map/all_to_all | solution.py:329
  40.0 0.0 copy-done.10
  40.0 0.1 maximum_bitcast_fusion
  40.1 0.0 copy-start.9
  40.1 0.1 copy.17.bias_ref
  40.2 0.6 copy-done.9
  40.8 0.1 fusion.2
  40.9 0.1 copy.16.point_ref
  41.0 0.0 copy-done
  41.0 0.0 copy-start.1
  41.0 1.1 shard_map.149
  42.1 0.0 copy-start.3
  42.1 0.8 copy-done.3
  42.9 0.0 copy-start.2
  42.9 0.0 copy-done.1
  42.9 0.3 shard_map.148.modes_ref
  43.2 8.9 %all-to-all-done.1 = bf16[8,512,128]{2,1,0:T(8,128)(2,1)S(1)} async-done(((bf16[8,512,128]{2,1,0:T(8,128)(2,1)}), bf16[8,512,128]{2,1,0:T(8,128)(2,1)S(1)}, u32[]{:S(2)}, u32[]{:S(2)}) %all-to-all-start.1) | async-done | bytes 1048608 | tf_op jit(solution)/shard_map/all_to_all | solution.py:329
  52.1 0.0 copy-done.2
  52.1 0.0 copy-start.4
  52.1 0.6 shard_map.151
  52.7 0.0 copy-start.6
  52.7 21.3 %all_to_all.67 = bf16[64,8,128]{2,1,0:T(8,128)(2,1)S(1)} all-to-all(bf16[64,8,128]{2,1,0:T(8,128)(2,1)S(1)} %bitcast.58), channel_id=1, replica_groups={{416,264,112,472,320,168,16,376,224,72,432,280,128,488,336,184,32,392,2..., dimensions={0} | all-to-all | bytes 262144 | tf_op jit(solution)/shard_map/all_to_all | solution.py:329
  74.1 0.0 copy-done.4
  74.1 0.0 copy-done.6
  74.1 1.1 shard_map.152
  75.1 20.4 %all_to_all.68 = bf16[64,8,128]{2,1,0:T(8,128)(2,1)S(1)} all-to-all(bf16[64,8,128]{2,1,0:T(8,128)(2,1)S(1)} %bitcast.63), channel_id=1, replica_groups={{416,264,112,472,320,168,16,376,224,72,432,280,128,488,336,184,32,392,2..., dimensions={0} | all-to-all | bytes 262144 | tf_op jit(solution)/shard_map/all_to_all | solution.py:329
  95.5 1.0 shard_map.153
  96.5 0.0 copy-start.5
  96.5 20.5 %all_to_all.69 = bf16[64,8,128]{2,1,0:T(8,128)(2,1)S(1)} all-to-all(bf16[64,8,128]{2,1,0:T(8,128)(2,1)S(1)} %bitcast.62), channel_id=1, replica_groups={{416,264,112,472,320,168,16,376,224,72,432,280,128,488,336,184,32,392,2..., dimensions={0} | all-to-all | bytes 262144 | tf_op jit(solution)/shard_map/all_to_all | solution.py:329
  117.1 7.2 %all-to-all-start.5 = ((bf16[8,16,128]{2,1,0:T(8,128)(2,1)}), bf16[8,16,128]{2,1,0:T(8,128)(2,1)S(1)}, u32[]{:S(2)}, u32[]{:S(2)}) async-start(bf16[8,16,128]{2,1,0:T(8,128)(2,1)} %bitcast.25), calls=%async_computation.5 | async-start | bytes 65536 | tf_op jit(solution)/shard_map/all_to_all | solution.py:329
  124.3 0.0 copy-done.5
  124.3 0.0 copy-start.7
  124.3 1.3 shard_map.154
  125.5 0.6 all-to-all-done.5
  126.1 0.0 copy-done.7
  126.2 1.5 %shard_map.155 = (f32[512,128]{1,0:T(8,128)}, f32[512,128]{1,0:T(8,128)}, f32[512,128]{1,0:T(8,128)}) custom-call(bf16[128,128]{1,0:T(8,128)(2,1)S(1)} %bitcast.61, bf16[256,128]{1,0:T(8,128)(2,1)S(1)} %copy-done.7, f32[512,128]{1,0:T(8,128)S(1)} %get-tuple-element.34.weight_ref, f32[512,128]{1,0:T(8,128)S(1)} %get-tuple-element.35.first_ref, ...), custom_call_target="tpu_custom_call" | custom-call | tf_op jit(solution)/shard_map/pallas_call | solution.py:317
Async XLA Ops:
  2.7 19.9 %copy-start.8 = (f32[8,1,2,4096]{3,2,1,0:T(2,128)S(1)}, f32[8,1,2,4096]{3,2,1,0:T(2,128)}, u32[]{:S(2)}) copy-start(f32[8,1,2,4096]{3,2,1,0:T(2,128)} %param.16) | copy-start | bytes 786436
  2.7 28.4 %all-to-all-start = ((bf16[64,8,128]{2,1,0:T(8,128)(2,1)}), bf16[64,8,128]{2,1,0:T(8,128)(2,1)S(1)}, u32[]{:S(2)}, u32[]{:S(2)}) async-start(bf16[64,8,128]{2,1,0:T(8,128)(2,1)} %bitcast.1), calls=%async_computation | async-start | bytes 262144 | tf_op jit(solution)/shard_map/all_to_all | solution.py:329
  31.1 8.9 %copy-start.10 = (f32[64]{0:T(128)S(1)}, f32[64]{0:T(128)}, u32[]{:S(2)}) copy-start(f32[64]{0:T(128)} %param.15) | copy-start | bytes 772
  31.1 9.9 %copy-start = (bf16[1,8,64,512]{3,2,1,0:T(8,128)(2,1)S(1)}, bf16[1,8,64,512]{3,2,1,0:T(8,128)(2,1)}, u32[]{:S(2)}) copy-start(bf16[1,8,64,512]{3,2,1,0:T(8,128)(2,1)} %param.12) | copy-start | bytes 1572868
  31.1 21.0 %all-to-all-start.1 = ((bf16[8,512,128]{2,1,0:T(8,128)(2,1)}), bf16[8,512,128]{2,1,0:T(8,128)(2,1)S(1)}, u32[]{:S(2)}, u32[]{:S(2)}) async-start(bf16[8,512,128]{2,1,0:T(8,128)(2,1)} %bitcast.7), calls=%async_computation.1 | async-start | bytes 2097152 | tf_op jit(solution)/shard_map/all_to_all | solution.py:329
  40.1 0.7 copy-start.9
  41.0 1.9 %copy-start.1 = (bf16[256,512]{1,0:T(8,128)(2,1)S(1)}, bf16[256,512]{1,0:T(8,128)(2,1)}, u32[]{:S(2)}) copy-start(bf16[256,512]{1,0:T(8,128)(2,1)} %constant.14.clone.to_modes_ref) | copy-start | bytes 786436
  42.1 0.8 copy-start.3
  42.9 9.2 %copy-start.2 = (bf16[512,256]{1,0:T(8,128)(2,1)S(1)}, bf16[512,256]{1,0:T(8,128)(2,1)}, u32[]{:S(2)}) copy-start(bf16[512,256]{1,0:T(8,128)(2,1)} %constant.15.clone.to_rows_ref) | copy-start | bytes 786436
  52.1 22.0 %copy-start.4 = (bf16[512,512]{1,0:T(8,128)(2,1)S(1)}, bf16[512,512]{1,0:T(8,128)(2,1)}, u32[]{:S(2)}) copy-start(bf16[512,512]{1,0:T(8,128)(2,1)} %copy-done.3) | copy-start | bytes 1572868
  52.7 21.3 %copy-start.6 = (bf16[128,512]{1,0:T(8,128)(2,1)S(1)}, bf16[128,512]{1,0:T(8,128)(2,1)}, u32[]{:S(2)}) copy-start(bf16[128,512]{1,0:T(8,128)(2,1)} %constant.13.clone.inverse_ref) | copy-start | bytes 393220
  96.5 27.8 %copy-start.5 = (bf16[128,512]{1,0:T(8,128)(2,1)S(1)}, bf16[128,512]{1,0:T(8,128)(2,1)}, u32[]{:S(2)}) copy-start(bf16[128,512]{1,0:T(8,128)(2,1)} %constant.12.clone.table_hbm.forward_ref) | copy-start | bytes 393220
  117.1 9.1 %all-to-all-start.5 = ((bf16[8,16,128]{2,1,0:T(8,128)(2,1)}), bf16[8,16,128]{2,1,0:T(8,128)(2,1)S(1)}, u32[]{:S(2)}, u32[]{:S(2)}) async-start(bf16[8,16,128]{2,1,0:T(8,128)(2,1)} %bitcast.25), calls=%async_computation.5 | async-start | bytes 65536 | tf_op jit(solution)/shard_map/all_to_all | solution.py:329
  124.3 1.9 %copy-start.7 = (bf16[256,128]{1,0:T(8,128)(2,1)S(1)}, bf16[256,128]{1,0:T(8,128)(2,1)}, u32[]{:S(2)}) copy-start(bf16[256,128]{1,0:T(8,128)(2,1)} %constant.16.clone.pick_ref) | copy-start | bytes 196612

commit v7 on v6

--- a/solution.py
+++ b/solution.py
@@ -18,7 +18,7 @@
 HALF = 64
 BLOCKS = 8
 
-GRID_ORDER = [(52 + 45 * k) % 64 for k in range(64)]
+GRID_ORDER = [(20 + 45 * k) % 64 for k in range(64)]
 DP_ORDER = [(5 + 3 * k) % 8 for k in range(8)]
 
 beta_one = 0.9

time: 129 us -> 129 us (level)
  waiting for transfers between devices: 16.1 us -> 17.4 us
    all_to_all x3, waiting for transfers between devices: 16.1 us -> 17.4 us  [exchange(): lax.all_to_all(array, axis, split_axis=0, concat_axis=0, axis_index_group...]
where the time goes in v7:
time: 129 us; the launch traced here: 128 us
  blocking collectives  61.6 us (48%)
  starting transfers between devices  35.6 us (28%)
  waiting for transfers between devices  17.4 us (13%)
  Pallas kernels  9.94 us (8%)
  local copies, waits for them, and re-layouts  2.29 us (2%)
    all_to_all x3, blocking collectives, exchange(): lax.all_to_all(array, axis, split_axis=0, concat_axis=0, axis_index_group...  61.6 us
    all_to_all x3, starting transfers between devices, exchange(): lax.all_to_all(array, axis, split_axis=0, concat_axis=0, axis_index_group...  35.6 us
    all_to_all x3, waiting for transfers between devices, exchange(): lax.all_to_all(array, axis, split_axis=0, concat_axis=0, axis_index_group...  17.4 us
    pallas_call x9, Pallas kernels, call(): pl.pallas_call(kernel, out_shape=[place(shape, dtype) for shape, dtype in...  9.94 us
  transfers between devices with their start and end apart: 3, of which 3 were waited for; matrix products, arithmetic and copies ran while one was open for 1% of the time, Pallas kernels for 3%

profile of v7, /device:TPU:1, one launch (start us, length us, event | category | flops | bytes accessed | tf_op | source)
XLA Modules:
  0.0 127.9 jit_solution(1529312958285780073)
XLA Ops:
  0.6 2.1 %shard_map.147 = bf16[512,128]{1,0:T(8,128)(2,1)} custom-call(bf16[512,512]{1,0:T(8,128)(2,1)} %bitcast.54, bf16[128,512]{1,0:T(8,128)(2,1)} %constant.12.clone.table_hbm.forward_ref), custom_call_target="tpu_custom_call" | custom-call | tf_op jit(solution)/shard_map/pallas_call | solution.py:317
  2.7 0.0 copy-start.8
  2.7 19.8 %all-to-all-start = ((bf16[64,8,128]{2,1,0:T(8,128)(2,1)}), bf16[64,8,128]{2,1,0:T(8,128)(2,1)S(1)}, u32[]{:S(2)}, u32[]{:S(2)}) async-start(bf16[64,8,128]{2,1,0:T(8,128)(2,1)} %bitcast.1), calls=%async_computation | async-start | bytes 262144 | tf_op jit(solution)/shard_map/all_to_all | solution.py:329
  22.5 0.0 copy-done.8
  22.5 0.1 convert_element_type.3
  22.6 0.2 reshape.77
  22.8 0.3 copy.26
  23.1 0.1 reshape.78.local_ref
  23.2 1.1 shard_map.150
  24.4 7.5 %all-to-all-done = bf16[64,8,128]{2,1,0:T(8,128)(2,1)S(1)} async-done(((bf16[64,8,128]{2,1,0:T(8,128)(2,1)}), bf16[64,8,128]{2,1,0:T(8,128)(2,1)S(1)}, u32[]{:S(2)}, u32[]{:S(2)}) %all-to-all-start) | async-done | bytes 131104 | tf_op jit(solution)/shard_map/all_to_all | solution.py:329
  31.9 0.0 copy-start.10
  31.9 0.0 copy-start
  31.9 8.7 %all-to-all-start.1 = ((bf16[8,512,128]{2,1,0:T(8,128)(2,1)}), bf16[8,512,128]{2,1,0:T(8,128)(2,1)S(1)}, u32[]{:S(2)}, u32[]{:S(2)}) async-start(bf16[8,512,128]{2,1,0:T(8,128)(2,1)} %bitcast.7), calls=%async_computation.1 | async-start | bytes 2097152 | tf_op jit(solution)/shard_map/all_to_all | solution.py:329
  40.6 0.0 copy-done.10
  40.6 0.1 maximum_bitcast_fusion
  40.7 0.0 copy-start.9
  40.7 0.1 copy.17.bias_ref
  40.8 0.6 copy-done.9
  41.4 0.1 fusion.2
  41.5 0.1 copy.16.point_ref
  41.6 0.0 copy-done
  41.6 0.0 copy-start.1
  41.6 1.1 shard_map.149
  42.7 0.0 copy-start.3
  42.7 0.8 copy-done.3
  43.5 0.0 copy-start.2
  43.5 0.0 copy-done.1
  43.5 0.3 shard_map.148.modes_ref
  43.8 9.3 %all-to-all-done.1 = bf16[8,512,128]{2,1,0:T(8,128)(2,1)S(1)} async-done(((bf16[8,512,128]{2,1,0:T(8,128)(2,1)}), bf16[8,512,128]{2,1,0:T(8,128)(2,1)S(1)}, u32[]{:S(2)}, u32[]{:S(2)}) %all-to-all-start.1) | async-done | bytes 1048608 | tf_op jit(solution)/shard_map/all_to_all | solution.py:329
  53.1 0.0 copy-done.2
  53.1 0.0 copy-start.4
  53.1 0.6 shard_map.151
  53.7 0.0 copy-start.6
  53.7 20.6 %all_to_all.67 = bf16[64,8,128]{2,1,0:T(8,128)(2,1)S(1)} all-to-all(bf16[64,8,128]{2,1,0:T(8,128)(2,1)S(1)} %bitcast.58), channel_id=1, replica_groups={{160,8,368,216,64,424,272,120,480,328,176,24,384,232,80,440,288,136,496..., dimensions={0} | all-to-all | bytes 262144 | tf_op jit(solution)/shard_map/all_to_all | solution.py:329
  74.3 0.0 copy-done.4
  74.3 0.0 copy-done.6
  74.4 1.1 shard_map.152
  75.4 20.4 %all_to_all.68 = bf16[64,8,128]{2,1,0:T(8,128)(2,1)S(1)} all-to-all(bf16[64,8,128]{2,1,0:T(8,128)(2,1)S(1)} %bitcast.63), channel_id=1, replica_groups={{160,8,368,216,64,424,272,120,480,328,176,24,384,232,80,440,288,136,496..., dimensions={0} | all-to-all | bytes 262144 | tf_op jit(solution)/shard_map/all_to_all | solution.py:329
  95.8 1.0 shard_map.153
  96.8 0.0 copy-start.5
  96.8 20.5 %all_to_all.69 = bf16[64,8,128]{2,1,0:T(8,128)(2,1)S(1)} all-to-all(bf16[64,8,128]{2,1,0:T(8,128)(2,1)S(1)} %bitcast.62), channel_id=1, replica_groups={{160,8,368,216,64,424,272,120,480,328,176,24,384,232,80,440,288,136,496..., dimensions={0} | all-to-all | bytes 262144 | tf_op jit(solution)/shard_map/all_to_all | solution.py:329
  117.4 7.2 %all-to-all-start.5 = ((bf16[8,16,128]{2,1,0:T(8,128)(2,1)}), bf16[8,16,128]{2,1,0:T(8,128)(2,1)S(1)}, u32[]{:S(2)}, u32[]{:S(2)}) async-start(bf16[8,16,128]{2,1,0:T(8,128)(2,1)} %bitcast.25), calls=%async_computation.5 | async-start | bytes 65536 | tf_op jit(solution)/shard_map/all_to_all | solution.py:329
  124.5 0.0 copy-done.5
  124.5 0.0 copy-start.7
  124.5 1.3 shard_map.154
  125.8 0.6 all-to-all-done.5
  126.4 0.0 copy-done.7
  126.4 1.5 %shard_map.155 = (f32[512,128]{1,0:T(8,128)}, f32[512,128]{1,0:T(8,128)}, f32[512,128]{1,0:T(8,128)}) custom-call(bf16[128,128]{1,0:T(8,128)(2,1)S(1)} %bitcast.61, bf16[256,128]{1,0:T(8,128)(2,1)S(1)} %copy-done.7, f32[512,128]{1,0:T(8,128)S(1)} %get-tuple-element.34.weight_ref, f32[512,128]{1,0:T(8,128)S(1)} %get-tuple-element.35.first_ref, ...), custom_call_target="tpu_custom_call" | custom-call | tf_op jit(solution)/shard_map/pallas_call | solution.py:317
Async XLA Ops:
  2.7 19.8 %copy-start.8 = (f32[8,1,2,4096]{3,2,1,0:T(2,128)S(1)}, f32[8,1,2,4096]{3,2,1,0:T(2,128)}, u32[]{:S(2)}) copy-start(f32[8,1,2,4096]{3,2,1,0:T(2,128)} %param.16) | copy-start | bytes 786436
  2.7 29.2 %all-to-all-start = ((bf16[64,8,128]{2,1,0:T(8,128)(2,1)}), bf16[64,8,128]{2,1,0:T(8,128)(2,1)S(1)}, u32[]{:S(2)}, u32[]{:S(2)}) async-start(bf16[64,8,128]{2,1,0:T(8,128)(2,1)} %bitcast.1), calls=%async_computation | async-start | bytes 262144 | tf_op jit(solution)/shard_map/all_to_all | solution.py:329
  31.9 8.7 %copy-start.10 = (f32[64]{0:T(128)S(1)}, f32[64]{0:T(128)}, u32[]{:S(2)}) copy-start(f32[64]{0:T(128)} %param.15) | copy-start | bytes 772
  31.9 9.7 %copy-start = (bf16[1,8,64,512]{3,2,1,0:T(8,128)(2,1)S(1)}, bf16[1,8,64,512]{3,2,1,0:T(8,128)(2,1)}, u32[]{:S(2)}) copy-start(bf16[1,8,64,512]{3,2,1,0:T(8,128)(2,1)} %param.12) | copy-start | bytes 1572868
  31.9 21.2 %all-to-all-start.1 = ((bf16[8,512,128]{2,1,0:T(8,128)(2,1)}), bf16[8,512,128]{2,1,0:T(8,128)(2,1)S(1)}, u32[]{:S(2)}, u32[]{:S(2)}) async-start(bf16[8,512,128]{2,1,0:T(8,128)(2,1)} %bitcast.7), calls=%async_computation.1 | async-start | bytes 2097152 | tf_op jit(solution)/shard_map/all_to_all | solution.py:329
  40.7 0.7 copy-start.9
  41.6 1.9 %copy-start.1 = (bf16[256,512]{1,0:T(8,128)(2,1)S(1)}, bf16[256,512]{1,0:T(8,128)(2,1)}, u32[]{:S(2)}) copy-start(bf16[256,512]{1,0:T(8,128)(2,1)} %constant.14.clone.to_modes_ref) | copy-start | bytes 786436
  42.7 0.8 copy-start.3
  43.5 9.6 %copy-start.2 = (bf16[512,256]{1,0:T(8,128)(2,1)S(1)}, bf16[512,256]{1,0:T(8,128)(2,1)}, u32[]{:S(2)}) copy-start(bf16[512,256]{1,0:T(8,128)(2,1)} %constant.15.clone.to_rows_ref) | copy-start | bytes 786436
  53.1 21.3 %copy-start.4 = (bf16[512,512]{1,0:T(8,128)(2,1)S(1)}, bf16[512,512]{1,0:T(8,128)(2,1)}, u32[]{:S(2)}) copy-start(bf16[512,512]{1,0:T(8,128)(2,1)} %copy-done.3) | copy-start | bytes 1572868
  53.7 20.7 %copy-start.6 = (bf16[128,512]{1,0:T(8,128)(2,1)S(1)}, bf16[128,512]{1,0:T(8,128)(2,1)}, u32[]{:S(2)}) copy-start(bf16[128,512]{1,0:T(8,128)(2,1)} %constant.13.clone.inverse_ref) | copy-start | bytes 393220
  96.8 27.7 %copy-start.5 = (bf16[128,512]{1,0:T(8,128)(2,1)S(1)}, bf16[128,512]{1,0:T(8,128)(2,1)}, u32[]{:S(2)}) copy-start(bf16[128,512]{1,0:T(8,128)(2,1)} %constant.12.clone.table_hbm.forward_ref) | copy-start | bytes 393220
  117.4 9.1 %all-to-all-start.5 = ((bf16[8,16,128]{2,1,0:T(8,128)(2,1)}), bf16[8,16,128]{2,1,0:T(8,128)(2,1)S(1)}, u32[]{:S(2)}, u32[]{:S(2)}) async-start(bf16[8,16,128]{2,1,0:T(8,128)(2,1)} %bitcast.25), calls=%async_computation.5 | async-start | bytes 65536 | tf_op jit(solution)/shard_map/all_to_all | solution.py:329
  124.5 1.9 %copy-start.7 = (bf16[256,128]{1,0:T(8,128)(2,1)S(1)}, bf16[256,128]{1,0:T(8,128)(2,1)}, u32[]{:S(2)}) copy-start(bf16[256,128]{1,0:T(8,128)(2,1)} %constant.16.clone.pick_ref) | copy-start | bytes 196612

commit v8 on v7

--- a/solution.py
+++ b/solution.py
@@ -251,8 +251,9 @@
         copy = pltpu.make_async_copy(out_ref.at[part(q)], out_hbm.at[part(q)], sems.at[q])
         copy.start()
         copies.append(copy)
-    for copy in loads + copies:
+    for copy in loads:
         copy.wait()
+    return copies
 
 
 def adam_kernel(
@@ -304,6 +305,61 @@
         copy.wait()
 
 
+def last_kernel(
+    received_ref,
+    grad_ref,
+    point_ref,
+    forward_ref,
+    weight_hbm,
+    first_hbm,
+    second_hbm,
+    pair_ref,
+    pick_ref,
+    out_hbm,
+    new_weight_hbm,
+    new_first_hbm,
+    new_second_hbm,
+    weight_ref,
+    first_ref,
+    second_ref,
+    out_ref,
+    woven_ref,
+    made_ref,
+    sems,
+    made_sems,
+):
+    copies = field_kernel(
+        received_ref,
+        grad_ref,
+        point_ref,
+        forward_ref,
+        weight_hbm,
+        first_hbm,
+        second_hbm,
+        out_hbm,
+        weight_ref,
+        first_ref,
+        second_ref,
+        out_ref,
+        woven_ref,
+        sems,
+    )
+    adam_kernel(
+        pair_ref,
+        pick_ref,
+        weight_ref,
+        first_ref,
+        second_ref,
+        new_weight_hbm,
+        new_first_hbm,
+        new_second_hbm,
+        made_ref,
+        made_sems,
+    )
+    for copy in copies:
+        copy.wait()
+
+
 HBM = pl.BlockSpec(memory_space=pltpu.HBM)
 VMEM = pl.BlockSpec(memory_space=pltpu.VMEM)
 
@@ -401,26 +457,29 @@
         for m in (spectral_weight, first_moment, second_moment)
     ]
     flat = [((512, 128), f32)] * 3
-    grad_field, *near = call(
-        field_kernel,
+    held = pltpu.VMEM((512, 128), f32)
+    grad_field, *made = call(
+        last_kernel,
         [((512, 512), bf16)] + flat,
         received,
         pre_grad,
         point,
         forward,
         *masters,
-        far=(4, 5, 6),
-        far_out=(0,),
-        scratch=(plane, woven, dma((QUAD + 3,))),
-    )
-    made = call(
-        adam_kernel,
-        flat,
         pair,
         pick,
-        *near,
-        far_out=(0, 1, 2),
-        scratch=(pltpu.VMEM((3, 512, 128), f32), dma((12,))),
+        far=(4, 5, 6),
+        far_out=(0, 1, 2, 3),
+        scratch=(
+            held,
+            held,
+            held,
+            plane,
+            woven,
+            pltpu.VMEM((3, 512, 128), f32),
+            dma((QUAD + 3,)),
+            dma((12,)),
+        ),
     )
     new_weight, new_first, new_second = (
         m.reshape(8, C // 2, 2, 128).transpose(0, 2, 1, 3).reshape(spectral_weight.shape)

time: 129 us -> 130 us (level)
  blocking collectives: 61.6 us -> 70.6 us
  starting transfers between devices: 35.6 us -> 28.4 us
  waiting for transfers between devices: 17.4 us -> 14.8 us
  local copies, waits for them, and re-layouts: 2.29 us -> 3.74 us
    all_to_all x3 -> x4, blocking collectives: 61.6 us -> 70.6 us  [exchange(): lax.all_to_all(array, axis, split_axis=0, concat_axis=0, axis_index_group...]
    all_to_all x3 -> x2, starting transfers between devices: 35.6 us -> 28.4 us  [exchange(): lax.all_to_all(array, axis, split_axis=0, concat_axis=0, axis_index_group...]
    all_to_all x3 -> x2, waiting for transfers between devices: 17.4 us -> 14.8 us  [exchange(): lax.all_to_all(array, axis, split_axis=0, concat_axis=0, axis_index_group...]
    pallas_call x9 -> x8, Pallas kernels: 9.94 us -> 9.86 us  [call(): pl.pallas_call(kernel, out_shape=[place(shape, dtype) for shape, dtype in...]
  transfers between devices with their start and end apart: 3 -> 2, of which waited for: 3 -> 2; matrix products, arithmetic and copies ran while one was open for 1% -> 2% of each run, Pallas kernels for 3% -> 2%
where the time goes in v8:
time: 130 us; the launch traced here: 129 us
  blocking collectives  70.6 us (54%)
  starting transfers between devices  28.4 us (22%)
  waiting for transfers between devices  14.8 us (11%)
  Pallas kernels  9.86 us (8%)
  local copies, waits for them, and re-layouts  3.74 us (3%)
    all_to_all x4, blocking collectives, exchange(): lax.all_to_all(array, axis, split_axis=0, concat_axis=0, axis_index_group...  70.6 us
    all_to_all x2, starting transfers between devices, exchange(): lax.all_to_all(array, axis, split_axis=0, concat_axis=0, axis_index_group...  28.4 us
    all_to_all x2, waiting for transfers between devices, exchange(): lax.all_to_all(array, axis, split_axis=0, concat_axis=0, axis_index_group...  14.8 us
    pallas_call x8, Pallas kernels, call(): pl.pallas_call(kernel, out_shape=[place(shape, dtype) for shape, dtype in...  9.86 us
  transfers between devices with their start and end apart: 2, of which 2 were waited for; matrix products, arithmetic and copies ran while one was open for 2% of the time, Pallas kernels for 2%

profile of v8, /device:TPU:1, one launch (start us, length us, event | category | flops | bytes accessed | tf_op | source)
XLA Modules:
  0.0 129.0 jit_solution(6744641171655049430)
XLA Ops:
  0.6 2.1 %shard_map.147 = bf16[512,128]{1,0:T(8,128)(2,1)} custom-call(bf16[512,512]{1,0:T(8,128)(2,1)} %bitcast.54, bf16[128,512]{1,0:T(8,128)(2,1)} %constant.12.clone.table_hbm.forward_ref), custom_call_target="tpu_custom_call" | custom-call | tf_op jit(solution)/shard_map/pallas_call | solution.py:373
  2.7 0.0 copy-start.9
  2.7 19.8 %all-to-all-start = ((bf16[64,8,128]{2,1,0:T(8,128)(2,1)}), bf16[64,8,128]{2,1,0:T(8,128)(2,1)S(1)}, u32[]{:S(2)}, u32[]{:S(2)}) async-start(bf16[64,8,128]{2,1,0:T(8,128)(2,1)} %bitcast.1), calls=%async_computation | async-start | bytes 262144 | tf_op jit(solution)/shard_map/all_to_all | solution.py:385
  22.5 0.0 copy-done.9
  22.5 0.1 convert_element_type.3
  22.6 0.2 reshape.77
  22.8 0.3 copy.26
  23.1 0.1 reshape.78.local_ref
  23.2 1.1 shard_map.150
  24.4 7.5 %all-to-all-done = bf16[64,8,128]{2,1,0:T(8,128)(2,1)S(1)} async-done(((bf16[64,8,128]{2,1,0:T(8,128)(2,1)}), bf16[64,8,128]{2,1,0:T(8,128)(2,1)S(1)}, u32[]{:S(2)}, u32[]{:S(2)}) %all-to-all-start) | async-done | bytes 131104 | tf_op jit(solution)/shard_map/all_to_all | solution.py:385
  31.9 0.0 copy-start.11
  31.9 0.0 copy-start
  31.9 8.7 %all-to-all-start.1 = ((bf16[8,512,128]{2,1,0:T(8,128)(2,1)}), bf16[8,512,128]{2,1,0:T(8,128)(2,1)S(1)}, u32[]{:S(2)}, u32[]{:S(2)}) async-start(bf16[8,512,128]{2,1,0:T(8,128)(2,1)} %bitcast.7), calls=%async_computation.1 | async-start | bytes 2097152 | tf_op jit(solution)/shard_map/all_to_all | solution.py:385
  40.6 0.0 copy-done.11
  40.6 0.1 maximum_bitcast_fusion
  40.7 0.0 copy-start.10
  40.7 0.7 copy.17.bias_ref
  41.4 0.0 copy-done.10
  41.4 0.7 fusion.2
  42.1 0.7 copy.16.point_ref
  42.8 0.0 copy-done
  42.8 0.0 copy-start.4
  42.8 0.8 copy-done.4
  43.7 0.0 copy-start.6
  43.7 0.8 copy-done.6
  44.4 0.0 copy-start.1
  44.4 1.1 shard_map.149
  45.5 0.0 copy-start.2
  45.5 0.0 copy-done.1
  45.6 0.3 shard_map.148.modes_ref
  45.8 7.3 %all-to-all-done.1 = bf16[8,512,128]{2,1,0:T(8,128)(2,1)S(1)} async-done(((bf16[8,512,128]{2,1,0:T(8,128)(2,1)}), bf16[8,512,128]{2,1,0:T(8,128)(2,1)S(1)}, u32[]{:S(2)}, u32[]{:S(2)}) %all-to-all-start.1) | async-done | bytes 1048608 | tf_op jit(solution)/shard_map/all_to_all | solution.py:385
  53.1 0.0 copy-done.2
  53.1 0.6 shard_map.151
  53.7 0.0 copy-start.5
  53.7 20.6 %all_to_all.67 = bf16[64,8,128]{2,1,0:T(8,128)(2,1)S(1)} all-to-all(bf16[64,8,128]{2,1,0:T(8,128)(2,1)S(1)} %bitcast.57), channel_id=1, replica_groups={{160,8,368,216,64,424,272,120,480,328,176,24,384,232,80,440,288,136,496..., dimensions={0} | all-to-all | bytes 262144 | tf_op jit(solution)/shard_map/all_to_all | solution.py:385
  74.3 0.0 copy-done.5
  74.3 1.1 shard_map.152
  75.4 20.4 %all_to_all.68 = bf16[64,8,128]{2,1,0:T(8,128)(2,1)S(1)} all-to-all(bf16[64,8,128]{2,1,0:T(8,128)(2,1)S(1)} %bitcast.62), channel_id=1, replica_groups={{160,8,368,216,64,424,272,120,480,328,176,24,384,232,80,440,288,136,496..., dimensions={0} | all-to-all | bytes 262144 | tf_op jit(solution)/shard_map/all_to_all | solution.py:385
  95.8 1.0 shard_map.153
  96.8 0.0 copy-start.3
  96.8 0.0 copy-start.8
  96.8 20.5 %all_to_all.69 = bf16[64,8,128]{2,1,0:T(8,128)(2,1)S(1)} all-to-all(bf16[64,8,128]{2,1,0:T(8,128)(2,1)S(1)} %bitcast.61), channel_id=1, replica_groups={{160,8,368,216,64,424,272,120,480,328,176,24,384,232,80,440,288,136,496..., dimensions={0} | all-to-all | bytes 262144 | tf_op jit(solution)/shard_map/all_to_all | solution.py:385
  117.4 0.0 copy-start.7
  117.4 9.0 %all_to_all.70 = bf16[8,16,128]{2,1,0:T(8,128)(2,1)S(1)} all-to-all(bf16[8,16,128]{2,1,0:T(8,128)(2,1)S(1)} %bitcast.64), channel_id=1, replica_groups={{5,0,3,6,1,4,7,2},{13,8,11,14,9,12,15,10},{21,16,19,22,17,20,23,18},{29..., dimensions={0} | all-to-all | bytes 65536 | tf_op jit(solution)/shard_map/all_to_all | solution.py:385
  126.3 0.0 copy-done.3
  126.3 0.0 copy-done.8
  126.3 0.0 copy-done.7
  126.4 2.7 %shard_map.154 = (bf16[512,512]{1,0:T(8,128)(2,1)}, f32[512,128]{1,0:T(8,128)}, f32[512,128]{1,0:T(8,128)}, f32[512,128]{1,0:T(8,128)}) custom-call(bf16[512,128]{1,0:T(8,128)(2,1)S(1)} %bitcast.59, bf16[512,512]{1,0:T(8,128)(2,1)S(1)} %get-tuple-element.28.grad_ref, bf16[128,128]{1,0:T(8,128)(2,1)S(1)} %copy-done.7, bf16[128,512]{1,0:T(8,128)(2,1)S(1)} %copy-done.3, ...), custom_call_target="tpu_custom_call" | custom-call | tf_op jit(solution)/shard_map/pallas_call | solution.py:373
Async XLA Ops:
  2.7 19.8 %copy-start.9 = (f32[8,1,2,4096]{3,2,1,0:T(2,128)S(1)}, f32[8,1,2,4096]{3,2,1,0:T(2,128)}, u32[]{:S(2)}) copy-start(f32[8,1,2,4096]{3,2,1,0:T(2,128)} %param.16) | copy-start | bytes 786436
  2.7 29.2 %all-to-all-start = ((bf16[64,8,128]{2,1,0:T(8,128)(2,1)}), bf16[64,8,128]{2,1,0:T(8,128)(2,1)S(1)}, u32[]{:S(2)}, u32[]{:S(2)}) async-start(bf16[64,8,128]{2,1,0:T(8,128)(2,1)} %bitcast.1), calls=%async_computation | async-start | bytes 262144 | tf_op jit(solution)/shard_map/all_to_all | solution.py:385
  31.9 8.7 %copy-start.11 = (f32[64]{0:T(128)S(1)}, f32[64]{0:T(128)}, u32[]{:S(2)}) copy-start(f32[64]{0:T(128)} %param.15) | copy-start | bytes 772
  31.9 10.9 %copy-start = (bf16[1,8,64,512]{3,2,1,0:T(8,128)(2,1)S(1)}, bf16[1,8,64,512]{3,2,1,0:T(8,128)(2,1)}, u32[]{:S(2)}) copy-start(bf16[1,8,64,512]{3,2,1,0:T(8,128)(2,1)} %param.12) | copy-start | bytes 1572868
  31.9 21.2 %all-to-all-start.1 = ((bf16[8,512,128]{2,1,0:T(8,128)(2,1)}), bf16[8,512,128]{2,1,0:T(8,128)(2,1)S(1)}, u32[]{:S(2)}, u32[]{:S(2)}) async-start(bf16[8,512,128]{2,1,0:T(8,128)(2,1)} %bitcast.7), calls=%async_computation.1 | async-start | bytes 2097152 | tf_op jit(solution)/shard_map/all_to_all | solution.py:385
  40.7 0.7 copy-start.10
  42.8 0.8 copy-start.4
  43.7 0.8 copy-start.6
  44.4 1.1 copy-start.1
  45.5 7.6 %copy-start.2 = (bf16[512,256]{1,0:T(8,128)(2,1)S(1)}, bf16[512,256]{1,0:T(8,128)(2,1)}, u32[]{:S(2)}) copy-start(bf16[512,256]{1,0:T(8,128)(2,1)} %constant.15.clone.to_rows_ref) | copy-start | bytes 786436
  53.7 20.6 %copy-start.5 = (bf16[128,512]{1,0:T(8,128)(2,1)S(1)}, bf16[128,512]{1,0:T(8,128)(2,1)}, u32[]{:S(2)}) copy-start(bf16[128,512]{1,0:T(8,128)(2,1)} %constant.13.clone.inverse_ref) | copy-start | bytes 393220
  96.8 29.5 %copy-start.3 = (bf16[128,512]{1,0:T(8,128)(2,1)S(1)}, bf16[128,512]{1,0:T(8,128)(2,1)}, u32[]{:S(2)}) copy-start(bf16[128,512]{1,0:T(8,128)(2,1)} %constant.12.clone.table_hbm.forward_ref) | copy-start | bytes 393220
  96.8 29.5 %copy-start.8 = (bf16[256,128]{1,0:T(8,128)(2,1)S(1)}, bf16[256,128]{1,0:T(8,128)(2,1)}, u32[]{:S(2)}) copy-start(bf16[256,128]{1,0:T(8,128)(2,1)} %constant.16.clone.pick_ref) | copy-start | bytes 196612
  117.4 9.0 %copy-start.7 = (bf16[128,128]{1,0:T(8,128)(2,1)S(1)}, bf16[128,128]{1,0:T(8,128)(2,1)}, u32[]{:S(2)}) copy-start(bf16[128,128]{1,0:T(8,128)(2,1)} %get-tuple-element.34.point_ref) | copy-start | bytes 98308

commit v9 on v7

--- a/solution.py
+++ b/solution.py
@@ -18,7 +18,7 @@
 HALF = 64
 BLOCKS = 8
 
-GRID_ORDER = [(20 + 45 * k) % 64 for k in range(64)]
+GRID_ORDER = [(20 + 25 * k) % 64 for k in range(64)]
 DP_ORDER = [(5 + 3 * k) % 8 for k in range(8)]
 
 beta_one = 0.9

time: 129 us -> 129 us (level)
  no operation moved by 1% of the time
where the time goes in v9:
time: 129 us; the launch traced here: 128 us
  blocking collectives  62.4 us (48%)
  starting transfers between devices  35.8 us (28%)
  waiting for transfers between devices  16.4 us (13%)
  Pallas kernels  9.95 us (8%)
  local copies, waits for them, and re-layouts  2.29 us (2%)
    all_to_all x3, blocking collectives, exchange(): lax.all_to_all(array, axis, split_axis=0, concat_axis=0, axis_index_group...  62.4 us
    all_to_all x3, starting transfers between devices, exchange(): lax.all_to_all(array, axis, split_axis=0, concat_axis=0, axis_index_group...  35.8 us
    all_to_all x3, waiting for transfers between devices, exchange(): lax.all_to_all(array, axis, split_axis=0, concat_axis=0, axis_index_group...  16.4 us
    pallas_call x9, Pallas kernels, call(): pl.pallas_call(kernel, out_shape=[place(shape, dtype) for shape, dtype in...  9.95 us
  transfers between devices with their start and end apart: 3, of which 3 were waited for; matrix products, arithmetic and copies ran while one was open for 1% of the time, Pallas kernels for 3%

profile of v9, /device:TPU:1, one launch (start us, length us, event | category | flops | bytes accessed | tf_op | source)
XLA Modules:
  0.0 127.8 jit_solution(17578370404166219645)
XLA Ops:
  0.6 2.1 %shard_map.147 = bf16[512,128]{1,0:T(8,128)(2,1)} custom-call(bf16[512,512]{1,0:T(8,128)(2,1)} %bitcast.54, bf16[128,512]{1,0:T(8,128)(2,1)} %constant.12.clone.table_hbm.forward_ref), custom_call_target="tpu_custom_call" | custom-call | tf_op jit(solution)/shard_map/pallas_call | solution.py:317
  2.7 0.0 copy-start.8
  2.7 20.0 %all-to-all-start = ((bf16[64,8,128]{2,1,0:T(8,128)(2,1)}), bf16[64,8,128]{2,1,0:T(8,128)(2,1)S(1)}, u32[]{:S(2)}, u32[]{:S(2)}) async-start(bf16[64,8,128]{2,1,0:T(8,128)(2,1)} %bitcast.1), calls=%async_computation | async-start | bytes 262144 | tf_op jit(solution)/shard_map/all_to_all | solution.py:329
  22.7 0.0 copy-done.8
  22.7 0.1 convert_element_type.3
  22.8 0.2 reshape.77
  23.1 0.3 copy.26
  23.3 0.1 reshape.78.local_ref
  23.5 1.1 shard_map.150
  24.6 7.2 %all-to-all-done = bf16[64,8,128]{2,1,0:T(8,128)(2,1)S(1)} async-done(((bf16[64,8,128]{2,1,0:T(8,128)(2,1)}), bf16[64,8,128]{2,1,0:T(8,128)(2,1)S(1)}, u32[]{:S(2)}, u32[]{:S(2)}) %all-to-all-start) | async-done | bytes 131104 | tf_op jit(solution)/shard_map/all_to_all | solution.py:329
  31.8 0.0 copy-start.10
  31.8 0.0 copy-start
  31.8 8.7 %all-to-all-start.1 = ((bf16[8,512,128]{2,1,0:T(8,128)(2,1)}), bf16[8,512,128]{2,1,0:T(8,128)(2,1)S(1)}, u32[]{:S(2)}, u32[]{:S(2)}) async-start(bf16[8,512,128]{2,1,0:T(8,128)(2,1)} %bitcast.7), calls=%async_computation.1 | async-start | bytes 2097152 | tf_op jit(solution)/shard_map/all_to_all | solution.py:329
  40.5 0.0 copy-done.10
  40.5 0.1 maximum_bitcast_fusion
  40.5 0.0 copy-start.9
  40.6 0.1 copy.17.bias_ref
  40.7 0.6 copy-done.9
  41.3 0.1 fusion.2
  41.3 0.1 copy.16.point_ref
  41.5 0.0 copy-done
  41.5 0.0 copy-start.1
  41.5 1.1 shard_map.149
  42.6 0.0 copy-start.3
  42.6 0.8 copy-done.3
  43.4 0.0 copy-start.2
  43.4 0.0 copy-done.1
  43.4 0.3 shard_map.148.modes_ref
  43.7 8.6 %all-to-all-done.1 = bf16[8,512,128]{2,1,0:T(8,128)(2,1)S(1)} async-done(((bf16[8,512,128]{2,1,0:T(8,128)(2,1)}), bf16[8,512,128]{2,1,0:T(8,128)(2,1)S(1)}, u32[]{:S(2)}, u32[]{:S(2)}) %all-to-all-start.1) | async-done | bytes 1048608 | tf_op jit(solution)/shard_map/all_to_all | solution.py:329
  52.3 0.0 copy-done.2
  52.3 0.0 copy-start.4
  52.3 0.6 shard_map.151
  52.9 0.0 copy-start.6
  52.9 21.6 %all_to_all.67 = bf16[64,8,128]{2,1,0:T(8,128)(2,1)S(1)} all-to-all(bf16[64,8,128]{2,1,0:T(8,128)(2,1)S(1)} %bitcast.58), channel_id=1, replica_groups={{160,360,48,248,448,136,336,24,224,424,112,312,0,200,400,88,288,488,176..., dimensions={0} | all-to-all | bytes 262144 | tf_op jit(solution)/shard_map/all_to_all | solution.py:329
  74.5 0.0 copy-done.4
  74.5 0.0 copy-done.6
  74.5 1.1 shard_map.152
  75.6 20.3 %all_to_all.68 = bf16[64,8,128]{2,1,0:T(8,128)(2,1)S(1)} all-to-all(bf16[64,8,128]{2,1,0:T(8,128)(2,1)S(1)} %bitcast.63), channel_id=1, replica_groups={{160,360,48,248,448,136,336,24,224,424,112,312,0,200,400,88,288,488,176..., dimensions={0} | all-to-all | bytes 262144 | tf_op jit(solution)/shard_map/all_to_all | solution.py:329
  95.9 1.0 shard_map.153
  96.9 0.0 copy-start.5
  96.9 20.5 %all_to_all.69 = bf16[64,8,128]{2,1,0:T(8,128)(2,1)S(1)} all-to-all(bf16[64,8,128]{2,1,0:T(8,128)(2,1)S(1)} %bitcast.62), channel_id=1, replica_groups={{160,360,48,248,448,136,336,24,224,424,112,312,0,200,400,88,288,488,176..., dimensions={0} | all-to-all | bytes 262144 | tf_op jit(solution)/shard_map/all_to_all | solution.py:329
  117.4 7.1 %all-to-all-start.5 = ((bf16[8,16,128]{2,1,0:T(8,128)(2,1)}), bf16[8,16,128]{2,1,0:T(8,128)(2,1)S(1)}, u32[]{:S(2)}, u32[]{:S(2)}) async-start(bf16[8,16,128]{2,1,0:T(8,128)(2,1)} %bitcast.25), calls=%async_computation.5 | async-start | bytes 65536 | tf_op jit(solution)/shard_map/all_to_all | solution.py:329
  124.5 0.0 copy-done.5
  124.5 0.0 copy-start.7
  124.5 1.3 shard_map.154
  125.7 0.6 all-to-all-done.5
  126.3 0.0 copy-done.7
  126.3 1.5 %shard_map.155 = (f32[512,128]{1,0:T(8,128)}, f32[512,128]{1,0:T(8,128)}, f32[512,128]{1,0:T(8,128)}) custom-call(bf16[128,128]{1,0:T(8,128)(2,1)S(1)} %bitcast.61, bf16[256,128]{1,0:T(8,128)(2,1)S(1)} %copy-done.7, f32[512,128]{1,0:T(8,128)S(1)} %get-tuple-element.34.weight_ref, f32[512,128]{1,0:T(8,128)S(1)} %get-tuple-element.35.first_ref, ...), custom_call_target="tpu_custom_call" | custom-call | tf_op jit(solution)/shard_map/pallas_call | solution.py:317
Async XLA Ops:
  2.7 20.0 %copy-start.8 = (f32[8,1,2,4096]{3,2,1,0:T(2,128)S(1)}, f32[8,1,2,4096]{3,2,1,0:T(2,128)}, u32[]{:S(2)}) copy-start(f32[8,1,2,4096]{3,2,1,0:T(2,128)} %param.16) | copy-start | bytes 786436
  2.7 29.1 %all-to-all-start = ((bf16[64,8,128]{2,1,0:T(8,128)(2,1)}), bf16[64,8,128]{2,1,0:T(8,128)(2,1)S(1)}, u32[]{:S(2)}, u32[]{:S(2)}) async-start(bf16[64,8,128]{2,1,0:T(8,128)(2,1)} %bitcast.1), calls=%async_computation | async-start | bytes 262144 | tf_op jit(solution)/shard_map/all_to_all | solution.py:329
  31.8 8.7 %copy-start.10 = (f32[64]{0:T(128)S(1)}, f32[64]{0:T(128)}, u32[]{:S(2)}) copy-start(f32[64]{0:T(128)} %param.15) | copy-start | bytes 772
  31.8 9.7 %copy-start = (bf16[1,8,64,512]{3,2,1,0:T(8,128)(2,1)S(1)}, bf16[1,8,64,512]{3,2,1,0:T(8,128)(2,1)}, u32[]{:S(2)}) copy-start(bf16[1,8,64,512]{3,2,1,0:T(8,128)(2,1)} %param.12) | copy-start | bytes 1572868
  31.8 20.5 %all-to-all-start.1 = ((bf16[8,512,128]{2,1,0:T(8,128)(2,1)}), bf16[8,512,128]{2,1,0:T(8,128)(2,1)S(1)}, u32[]{:S(2)}, u32[]{:S(2)}) async-start(bf16[8,512,128]{2,1,0:T(8,128)(2,1)} %bitcast.7), calls=%async_computation.1 | async-start | bytes 2097152 | tf_op jit(solution)/shard_map/all_to_all | solution.py:329
  40.5 0.7 copy-start.9
  41.5 1.9 %copy-start.1 = (bf16[256,512]{1,0:T(8,128)(2,1)S(1)}, bf16[256,512]{1,0:T(8,128)(2,1)}, u32[]{:S(2)}) copy-start(bf16[256,512]{1,0:T(8,128)(2,1)} %constant.14.clone.to_modes_ref) | copy-start | bytes 786436
  42.6 0.8 copy-start.3
  43.4 8.9 %copy-start.2 = (bf16[512,256]{1,0:T(8,128)(2,1)S(1)}, bf16[512,256]{1,0:T(8,128)(2,1)}, u32[]{:S(2)}) copy-start(bf16[512,256]{1,0:T(8,128)(2,1)} %constant.15.clone.to_rows_ref) | copy-start | bytes 786436
  52.3 22.2 %copy-start.4 = (bf16[512,512]{1,0:T(8,128)(2,1)S(1)}, bf16[512,512]{1,0:T(8,128)(2,1)}, u32[]{:S(2)}) copy-start(bf16[512,512]{1,0:T(8,128)(2,1)} %copy-done.3) | copy-start | bytes 1572868
  52.9 21.6 %copy-start.6 = (bf16[128,512]{1,0:T(8,128)(2,1)S(1)}, bf16[128,512]{1,0:T(8,128)(2,1)}, u32[]{:S(2)}) copy-start(bf16[128,512]{1,0:T(8,128)(2,1)} %constant.13.clone.inverse_ref) | copy-start | bytes 393220
  96.9 27.6 %copy-start.5 = (bf16[128,512]{1,0:T(8,128)(2,1)S(1)}, bf16[128,512]{1,0:T(8,128)(2,1)}, u32[]{:S(2)}) copy-start(bf16[128,512]{1,0:T(8,128)(2,1)} %constant.12.clone.table_hbm.forward_ref) | copy-start | bytes 393220
  117.4 9.0 %all-to-all-start.5 = ((bf16[8,16,128]{2,1,0:T(8,128)(2,1)}), bf16[8,16,128]{2,1,0:T(8,128)(2,1)S(1)}, u32[]{:S(2)}, u32[]{:S(2)}) async-start(bf16[8,16,128]{2,1,0:T(8,128)(2,1)} %bitcast.25), calls=%async_computation.5 | async-start | bytes 65536 | tf_op jit(solution)/shard_map/all_to_all | solution.py:329
  124.5 1.9 %copy-start.7 = (bf16[256,128]{1,0:T(8,128)(2,1)S(1)}, bf16[256,128]{1,0:T(8,128)(2,1)}, u32[]{:S(2)}) copy-start(bf16[256,128]{1,0:T(8,128)(2,1)} %constant.16.clone.pick_ref) | copy-start | bytes 196612
